TPU v7x, 128 devices: a whole 4x4x4 slice. The times are simulated.
128 devices in a mesh: seq: 8 (over y, z_hi), blk: 16 (over z_lo, x, core).
Axes of the slice: x: 4, y: 4, z: 4 (z_hi: 2, z_lo: 2; z = z_hi * 2 + z_lo), core: 2. Of those that a mesh axis runs over, the one named last changes fastest.
Arguments:
- queries: bfloat16 [8192, 8192], P(('seq', 'blk')), may hold values from -72 to 72
- keys: bfloat16 [8192, 1024], P(('seq', 'blk')), may hold values from -6 to 6
- values: bfloat16 [8192, 1024], P(('seq', 'blk')), may hold values from -8 to 8
Outputs:
- attended: bfloat16 [8192, 8192], P(('seq', 'blk'))
All inputs are finite; a program needn't handle non-finite values.
Results may differ from a plain program's by a relative error of at most 0.012.
Values may be sent and summed in bfloat16 or wider, within the bound.
No kernel may reach another device: no remote copies, remote signals or barrier semaphores. Data moves between devices by JAX's collectives and lax.ppermute only.
A program may use at most 128 MiB of HBM per device.

v0:
```python
import math

import jax
import jax.numpy as jnp
from jax import lax
from jax.sharding import PartitionSpec as P

HEAD_DIM = 128


def sylvester(order_size):
    indices = jnp.arange(order_size, dtype=jnp.int32)
    parity = jnp.zeros((order_size, order_size), jnp.int32)
    for bit_pos in range(order_size.bit_length() - 1):
        parity = parity + (indices[:, None] >> bit_pos & 1) * (indices[None, :] >> bit_pos & 1)
    return (1 - 2 * (parity % 2)).astype(jnp.bfloat16)


def rotate(matrix, order_size):
    head_count = matrix.shape[1] // order_size
    flattened = matrix.reshape(matrix.shape[0] * head_count, order_size)
    turned = jnp.dot(
        flattened, sylvester(order_size), preferred_element_type=jnp.float32
    ) * order_size ** (-0.5)
    return turned.astype(jnp.bfloat16).reshape(matrix.shape)


def starting_carry(query_group_count):
    shape_rows = query_group_count.shape[:3]
    return (
        jnp.full(shape_rows, -1e30, jnp.float32),
        jnp.zeros(shape_rows, jnp.float32),
        jnp.zeros(query_group_count.shape, jnp.float32),
    )


def finish(folded, row_count):
    run_max, run_sum, run_out = folded
    return (run_out / run_sum[..., None]).astype(jnp.bfloat16).reshape(row_count, -1)


def make_fold(query_group_count, query_pos, key_position, folded, shard_piece):
    kv_heads = query_group_count.shape[1]
    head_width = query_group_count.shape[3]
    score_scale = head_width ** (-0.5)
    key_rows, value_rows = shard_piece
    total_rows = key_rows.shape[0]
    block_size = math.gcd(total_rows, 512)
    blocks = total_rows // block_size
    key_blocks = key_rows.reshape(blocks, block_size, kv_heads, head_width)
    value_blocks = value_rows.reshape(blocks, block_size, kv_heads, head_width)
    firsts = jnp.arange(blocks, dtype=jnp.int32) * block_size

    def advance(running, block_item):
        run_max, run_sum, run_out = running
        block_of_keys, block_of_values, first_row = block_item
        key_pos = key_position(first_row + jnp.arange(block_size, dtype=jnp.int32))
        scores = (
            jnp.einsum(
                "foty,loy->fotl",
                query_group_count,
                block_of_keys,
                preferred_element_type=jnp.float32,
            )
            * score_scale
        )
        visible = key_pos[None, :] <= query_pos[:, None]
        scores = jnp.where(visible[:, None, None, :], scores, -jnp.inf)
        new_max = jnp.maximum(run_max, jnp.max(scores, axis=-1))
        weights = jnp.exp(scores - new_max[..., None])
        factor = jnp.exp(run_max - new_max)
        new_sum = run_sum * factor + jnp.sum(weights, axis=-1)
        update = jnp.einsum(
            "otzp,pth->otzh",
            weights.astype(jnp.bfloat16),
            block_of_values,
            preferred_element_type=jnp.float32,
        )
        return ((new_max, new_sum, run_out * factor[..., None] + update), None)

    folded, unused = lax.scan(advance, folded, (key_blocks, value_blocks, firsts))
    return folded


def on_device(queries, keys, values):
    head_width = HEAD_DIM
    n_blk = lax.axis_size("blk")
    tok_rows = queries.shape[0]
    rotated_keys = rotate(keys, head_width)
    rotated_values = rotate(values, head_width)
    blk_index = lax.axis_index("blk")
    head_queries, head_keys, head_values = (
        lax.all_to_all(queries, "seq", split_axis=1, concat_axis=0, tiled=True),
        lax.all_to_all(rotated_keys, "seq", split_axis=1, concat_axis=0, tiled=True),
        lax.all_to_all(rotated_values, "seq", split_axis=1, concat_axis=0, tiled=True),
    )
    rows_here = head_queries.shape[0]
    key_value_resident = head_keys.shape[1] // head_width
    query_group_count = head_queries.reshape(
        rows_here,
        key_value_resident,
        head_queries.shape[1] // head_width // key_value_resident,
        head_width,
    )
    local_rows = jnp.arange(rows_here, dtype=jnp.int32)
    query_pos = (local_rows // tok_rows * n_blk + blk_index) * tok_rows + local_rows % tok_rows

    def key_position(gathered):
        within = gathered % rows_here
        return (within // tok_rows * n_blk + gathered // rows_here) * tok_rows + within % tok_rows

    folded = make_fold(
        query_group_count,
        query_pos,
        key_position,
        starting_carry(query_group_count),
        (
            lax.all_gather(head_keys, "blk", axis=0, tiled=True),
            lax.all_gather(head_values, "blk", axis=0, tiled=True),
        ),
    )
    return lax.all_to_all(finish(folded, rows_here), "seq", split_axis=0, concat_axis=1, tiled=True)


def solution(mesh):
    in_specs = (P(("seq", "blk"), None), P(("seq", "blk"), None), P(("seq", "blk"), None))
    out_specs = P(("seq", "blk"), None)
    return jax.shard_map(
        on_device, mesh=mesh, in_specs=in_specs, out_specs=out_specs, check_vma=False
    )
```

profile of v0, /device:TPU:0, one launch (start us, length us, event | category | flops | bytes accessed | tf_op | source)
XLA Modules:
  0.0 375.2 jit_solution(4882414067634888757)
XLA Ops:
  8.2 15.7 %all_to_all.73 = bf16[64,8,128]{2,0,1:T(8,128)(2,1)} all-to-all(bf16[64,8,128]{2,0,1:T(8,128)(2,1)S(1)} %copy.32), channel_id=1, replica_groups=mesh['seq'=8,'blk'=16] {'seq'}, dimensions={1} | all-to-all | bytes 262144 | tf_op jit(solution)/shard_map/all_to_all | solution.py:95
  25.4 11.0 %all_to_all.74 = bf16[64,8,128]{2,0,1:T(8,128)(2,1)} all-to-all(bf16[64,8,128]{2,0,1:T(8,128)(2,1)S(1)} %copy.29), channel_id=1, replica_groups=mesh['seq'=8,'blk'=16] {'seq'}, dimensions={1} | all-to-all | bytes 262144 | tf_op jit(solution)/shard_map/all_to_all | solution.py:94
  41.1 16.2 %all-to-all-done.1 = bf16[64,8,1024]{2,0,1:T(8,128)(2,1)S(1)} async-done(((bf16[64,8,1024]{2,0,1:T(8,128)(2,1)}), bf16[64,8,1024]{2,0,1:T(8,128)(2,1)S(1)}, u32[]{:S(2)}, u32[]{:S(2)}) %all-to-all-start.1) | async-done | bytes 1048608 | tf_op jit(solution)/shard_map/all_to_all | solution.py:93
  57.8 5.6 %all-gather.5.cloned.1.call-done = bf16[8192,128]{1,0:T(8,128)(2,1)} async-done(((bf16[512,128]{1,0:T(8,128)(2,1)}), bf16[8192,128]{1,0:T(8,128)(2,1)}) %all-gather.5.cloned.1.call-update) | async-done | bytes 2097168 | tf_op jit(solution)/shard_map/all_gather | solution.py:119
  63.4 36.8 %all-gather.3.cloned.1.call-done = bf16[8192,128]{1,0:T(8,128)(2,1)} async-done(((bf16[512,128]{1,0:T(8,128)(2,1)}), bf16[8192,128]{1,0:T(8,128)(2,1)}) %all-gather.3.cloned.1.call-update) | async-done | bytes 2097168 | tf_op jit(solution)/shard_map/all_gather | solution.py:118
  100.2 242.0 %while.18 = (s32[]{:T(128)}, f32[512,1,8]{0,2,1:T(8,128)S(1)}, f32[512,1,8]{0,2,1:T(8,128)S(1)}, f32[512,1,8,128]{0,3,2,1:T(8,128)S(1)}, s32[16]{0:T(128)S(1)}, ...) while((s32[]{:T(128)}, f32[512,1,8]{0,2,1:T(8,128)S(1)}, ...), condition=%wide.region_3.4_spmd.clone, body=%wide.region_0.3_spmd.clone.sunk | while | flops 1098700288 | bytes 65545384 | solution.py:81
  107.2 6.3 %bitcast_add_fusion.5 = f32[512,1,8,128]{0,3,2,1:T(8,128)S(1)} fusion(f32[512,1,8,128]{0,3,2,1:T(8,128)S(1)} %get-tuple-element.334, f32[512,512,8]{1,0,2:T(8,128)} %get-tuple-element.318, f32[512,8]{0,1:T(8,128)S(1)} %bitcast.111, pred[512,512]{0,1:T(8,128)(4,1)S(1)} %broadcast_compare_fusion.2, f32[512,8]{0,1:T(8,128)S(1)} %get-tuple-element.319, ...), kind=kOutput, calls=%fused_computation.9.clone.1 | convolution fusion | flops 546832384 | bytes 13009409 | tf_op jit(solution)/shard_map/while/body/eval_jaxpr/otzp,pth->otzh/dot_general | solution.py:73
  122.4 6.3 %bitcast_add_fusion.5 = f32[512,1,8,128]{0,3,2,1:T(8,128)S(1)} fusion(f32[512,1,8,128]{0,3,2,1:T(8,128)S(1)} %get-tuple-element.334, f32[512,512,8]{1,0,2:T(8,128)} %get-tuple-element.318, f32[512,8]{0,1:T(8,128)S(1)} %bitcast.111, pred[512,512]{0,1:T(8,128)(4,1)S(1)} %broadcast_compare_fusion.2, f32[512,8]{0,1:T(8,128)S(1)} %get-tuple-element.319, ...), kind=kOutput, calls=%fused_computation.9.clone.1 | convolution fusion | flops 546832384 | bytes 13009409 | tf_op jit(solution)/shard_map/while/body/eval_jaxpr/otzp,pth->otzh/dot_general | solution.py:73
  137.5 6.3 %bitcast_add_fusion.5 = f32[512,1,8,128]{0,3,2,1:T(8,128)S(1)} fusion(f32[512,1,8,128]{0,3,2,1:T(8,128)S(1)} %get-tuple-element.334, f32[512,512,8]{1,0,2:T(8,128)} %get-tuple-element.318, f32[512,8]{0,1:T(8,128)S(1)} %bitcast.111, pred[512,512]{0,1:T(8,128)(4,1)S(1)} %broadcast_compare_fusion.2, f32[512,8]{0,1:T(8,128)S(1)} %get-tuple-element.319, ...), kind=kOutput, calls=%fused_computation.9.clone.1 | convolution fusion | flops 546832384 | bytes 13009409 | tf_op jit(solution)/shard_map/while/body/eval_jaxpr/otzp,pth->otzh/dot_general | solution.py:73
  152.6 6.3 %bitcast_add_fusion.5 = f32[512,1,8,128]{0,3,2,1:T(8,128)S(1)} fusion(f32[512,1,8,128]{0,3,2,1:T(8,128)S(1)} %get-tuple-element.334, f32[512,512,8]{1,0,2:T(8,128)} %get-tuple-element.318, f32[512,8]{0,1:T(8,128)S(1)} %bitcast.111, pred[512,512]{0,1:T(8,128)(4,1)S(1)} %broadcast_compare_fusion.2, f32[512,8]{0,1:T(8,128)S(1)} %get-tuple-element.319, ...), kind=kOutput, calls=%fused_computation.9.clone.1 | convolution fusion | flops 546832384 | bytes 13009409 | tf_op jit(solution)/shard_map/while/body/eval_jaxpr/otzp,pth->otzh/dot_general | solution.py:73
  167.7 6.3 %bitcast_add_fusion.5 = f32[512,1,8,128]{0,3,2,1:T(8,128)S(1)} fusion(f32[512,1,8,128]{0,3,2,1:T(8,128)S(1)} %get-tuple-element.334, f32[512,512,8]{1,0,2:T(8,128)} %get-tuple-element.318, f32[512,8]{0,1:T(8,128)S(1)} %bitcast.111, pred[512,512]{0,1:T(8,128)(4,1)S(1)} %broadcast_compare_fusion.2, f32[512,8]{0,1:T(8,128)S(1)} %get-tuple-element.319, ...), kind=kOutput, calls=%fused_computation.9.clone.1 | convolution fusion | flops 546832384 | bytes 13009409 | tf_op jit(solution)/shard_map/while/body/eval_jaxpr/otzp,pth->otzh/dot_general | solution.py:73
  182.9 6.3 %bitcast_add_fusion.5 = f32[512,1,8,128]{0,3,2,1:T(8,128)S(1)} fusion(f32[512,1,8,128]{0,3,2,1:T(8,128)S(1)} %get-tuple-element.334, f32[512,512,8]{1,0,2:T(8,128)} %get-tuple-element.318, f32[512,8]{0,1:T(8,128)S(1)} %bitcast.111, pred[512,512]{0,1:T(8,128)(4,1)S(1)} %broadcast_compare_fusion.2, f32[512,8]{0,1:T(8,128)S(1)} %get-tuple-element.319, ...), kind=kOutput, calls=%fused_computation.9.clone.1 | convolution fusion | flops 546832384 | bytes 13009409 | tf_op jit(solution)/shard_map/while/body/eval_jaxpr/otzp,pth->otzh/dot_general | solution.py:73
  198.0 6.3 %bitcast_add_fusion.5 = f32[512,1,8,128]{0,3,2,1:T(8,128)S(1)} fusion(f32[512,1,8,128]{0,3,2,1:T(8,128)S(1)} %get-tuple-element.334, f32[512,512,8]{1,0,2:T(8,128)} %get-tuple-element.318, f32[512,8]{0,1:T(8,128)S(1)} %bitcast.111, pred[512,512]{0,1:T(8,128)(4,1)S(1)} %broadcast_compare_fusion.2, f32[512,8]{0,1:T(8,128)S(1)} %get-tuple-element.319, ...), kind=kOutput, calls=%fused_computation.9.clone.1 | convolution fusion | flops 546832384 | bytes 13009409 | tf_op jit(solution)/shard_map/while/body/eval_jaxpr/otzp,pth->otzh/dot_general | solution.py:73
  213.1 6.3 %bitcast_add_fusion.5 = f32[512,1,8,128]{0,3,2,1:T(8,128)S(1)} fusion(f32[512,1,8,128]{0,3,2,1:T(8,128)S(1)} %get-tuple-element.334, f32[512,512,8]{1,0,2:T(8,128)} %get-tuple-element.318, f32[512,8]{0,1:T(8,128)S(1)} %bitcast.111, pred[512,512]{0,1:T(8,128)(4,1)S(1)} %broadcast_compare_fusion.2, f32[512,8]{0,1:T(8,128)S(1)} %get-tuple-element.319, ...), kind=kOutput, calls=%fused_computation.9.clone.1 | convolution fusion | flops 546832384 | bytes 13009409 | tf_op jit(solution)/shard_map/while/body/eval_jaxpr/otzp,pth->otzh/dot_general | solution.py:73
  222.7 5.5 %fusion.68 = (f32[512,8]{0,1:T(8,128)S(1)}, f32[512,512,8]{1,0,2:T(8,128)}) fusion(pred[512,512]{0,1:T(8,128)(4,1)S(1)} %broadcast_compare_fusion.2, bf16[512,1,8,128]{3,0,2,1:T(8,128)(2,1)S(1)} %get-tuple-element.348, bf16[16,512,1,128]{3,1,2,0:T(8,128)(2,1)} %get-tuple-element.347, s32[]{:T(128)} %get-tuple-element.331), kind=kOutput, calls=%fused_computation.5.clone.1 | convolution fusion | flops 543158272 | bytes 9847296 | tf_op jit(solution)/shard_map/while/body/eval_jaxpr/foty,loy->fotl/dot_general | solution.py:59
  228.2 6.3 %bitcast_add_fusion.5 = f32[512,1,8,128]{0,3,2,1:T(8,128)S(1)} fusion(f32[512,1,8,128]{0,3,2,1:T(8,128)S(1)} %get-tuple-element.334, f32[512,512,8]{1,0,2:T(8,128)} %get-tuple-element.318, f32[512,8]{0,1:T(8,128)S(1)} %bitcast.111, pred[512,512]{0,1:T(8,128)(4,1)S(1)} %broadcast_compare_fusion.2, f32[512,8]{0,1:T(8,128)S(1)} %get-tuple-element.319, ...), kind=kOutput, calls=%fused_computation.9.clone.1 | convolution fusion | flops 546832384 | bytes 13009409 | tf_op jit(solution)/shard_map/while/body/eval_jaxpr/otzp,pth->otzh/dot_general | solution.py:73
  243.4 6.3 %bitcast_add_fusion.5 = f32[512,1,8,128]{0,3,2,1:T(8,128)S(1)} fusion(f32[512,1,8,128]{0,3,2,1:T(8,128)S(1)} %get-tuple-element.334, f32[512,512,8]{1,0,2:T(8,128)} %get-tuple-element.318, f32[512,8]{0,1:T(8,128)S(1)} %bitcast.111, pred[512,512]{0,1:T(8,128)(4,1)S(1)} %broadcast_compare_fusion.2, f32[512,8]{0,1:T(8,128)S(1)} %get-tuple-element.319, ...), kind=kOutput, calls=%fused_computation.9.clone.1 | convolution fusion | flops 546832384 | bytes 13009409 | tf_op jit(solution)/shard_map/while/body/eval_jaxpr/otzp,pth->otzh/dot_general | solution.py:73
  258.5 6.3 %bitcast_add_fusion.5 = f32[512,1,8,128]{0,3,2,1:T(8,128)S(1)} fusion(f32[512,1,8,128]{0,3,2,1:T(8,128)S(1)} %get-tuple-element.334, f32[512,512,8]{1,0,2:T(8,128)} %get-tuple-element.318, f32[512,8]{0,1:T(8,128)S(1)} %bitcast.111, pred[512,512]{0,1:T(8,128)(4,1)S(1)} %broadcast_compare_fusion.2, f32[512,8]{0,1:T(8,128)S(1)} %get-tuple-element.319, ...), kind=kOutput, calls=%fused_computation.9.clone.1 | convolution fusion | flops 546832384 | bytes 13009409 | tf_op jit(solution)/shard_map/while/body/eval_jaxpr/otzp,pth->otzh/dot_general | solution.py:73
  273.6 6.3 %bitcast_add_fusion.5 = f32[512,1,8,128]{0,3,2,1:T(8,128)S(1)} fusion(f32[512,1,8,128]{0,3,2,1:T(8,128)S(1)} %get-tuple-element.334, f32[512,512,8]{1,0,2:T(8,128)} %get-tuple-element.318, f32[512,8]{0,1:T(8,128)S(1)} %bitcast.111, pred[512,512]{0,1:T(8,128)(4,1)S(1)} %broadcast_compare_fusion.2, f32[512,8]{0,1:T(8,128)S(1)} %get-tuple-element.319, ...), kind=kOutput, calls=%fused_computation.9.clone.1 | convolution fusion | flops 546832384 | bytes 13009409 | tf_op jit(solution)/shard_map/while/body/eval_jaxpr/otzp,pth->otzh/dot_general | solution.py:73
  288.7 6.3 %bitcast_add_fusion.5 = f32[512,1,8,128]{0,3,2,1:T(8,128)S(1)} fusion(f32[512,1,8,128]{0,3,2,1:T(8,128)S(1)} %get-tuple-element.334, f32[512,512,8]{1,0,2:T(8,128)} %get-tuple-element.318, f32[512,8]{0,1:T(8,128)S(1)} %bitcast.111, pred[512,512]{0,1:T(8,128)(4,1)S(1)} %broadcast_compare_fusion.2, f32[512,8]{0,1:T(8,128)S(1)} %get-tuple-element.319, ...), kind=kOutput, calls=%fused_computation.9.clone.1 | convolution fusion | flops 546832384 | bytes 13009409 | tf_op jit(solution)/shard_map/while/body/eval_jaxpr/otzp,pth->otzh/dot_general | solution.py:73
  303.9 6.3 %bitcast_add_fusion.5 = f32[512,1,8,128]{0,3,2,1:T(8,128)S(1)} fusion(f32[512,1,8,128]{0,3,2,1:T(8,128)S(1)} %get-tuple-element.334, f32[512,512,8]{1,0,2:T(8,128)} %get-tuple-element.318, f32[512,8]{0,1:T(8,128)S(1)} %bitcast.111, pred[512,512]{0,1:T(8,128)(4,1)S(1)} %broadcast_compare_fusion.2, f32[512,8]{0,1:T(8,128)S(1)} %get-tuple-element.319, ...), kind=kOutput, calls=%fused_computation.9.clone.1 | convolution fusion | flops 546832384 | bytes 13009409 | tf_op jit(solution)/shard_map/while/body/eval_jaxpr/otzp,pth->otzh/dot_general | solution.py:73
  319.0 6.3 %bitcast_add_fusion.5 = f32[512,1,8,128]{0,3,2,1:T(8,128)S(1)} fusion(f32[512,1,8,128]{0,3,2,1:T(8,128)S(1)} %get-tuple-element.334, f32[512,512,8]{1,0,2:T(8,128)} %get-tuple-element.318, f32[512,8]{0,1:T(8,128)S(1)} %bitcast.111, pred[512,512]{0,1:T(8,128)(4,1)S(1)} %broadcast_compare_fusion.2, f32[512,8]{0,1:T(8,128)S(1)} %get-tuple-element.319, ...), kind=kOutput, calls=%fused_computation.9.clone.1 | convolution fusion | flops 546832384 | bytes 13009409 | tf_op jit(solution)/shard_map/while/body/eval_jaxpr/otzp,pth->otzh/dot_general | solution.py:73
  334.1 6.3 %bitcast_add_fusion.5 = f32[512,1,8,128]{0,3,2,1:T(8,128)S(1)} fusion(f32[512,1,8,128]{0,3,2,1:T(8,128)S(1)} %get-tuple-element.334, f32[512,512,8]{1,0,2:T(8,128)} %get-tuple-element.318, f32[512,8]{0,1:T(8,128)S(1)} %bitcast.111, pred[512,512]{0,1:T(8,128)(4,1)S(1)} %broadcast_compare_fusion.2, f32[512,8]{0,1:T(8,128)S(1)} %get-tuple-element.319, ...), kind=kOutput, calls=%fused_computation.9.clone.1 | convolution fusion | flops 546832384 | bytes 13009409 | tf_op jit(solution)/shard_map/while/body/eval_jaxpr/otzp,pth->otzh/dot_general | solution.py:73
  343.8 23.5 %all_to_all.75 = bf16[8,64,1024]{2,1,0:T(8,128)(2,1)S(1)} all-to-all(bf16[8,64,1024]{2,1,0:T(8,128)(2,1)S(1)} %all_to_all.65), channel_id=1, replica_groups=mesh['seq'=8,'blk'=16] {'seq'}, dimensions={0} | all-to-all | bytes 2097152 | tf_op jit(solution)/shard_map/all_to_all | solution.py:122
  (189 shorter events, 145.2 us)
Async XLA Ops:
  6.5 29.9 %copy-start.1 = (bf16[64,8192]{1,0:T(8,128)(2,1)S(1)}, bf16[64,8192]{1,0:T(8,128)(2,1)}, u32[]{:S(2)}) copy-start(bf16[64,8192]{1,0:T(8,128)(2,1)} %param.5) | copy-start | bytes 3145732
  6.5 56.9 %all-gather.5.cloned.1.call-start = ((), (), s32[]{:S(2)}) async-start(), calls=%async_computation.5 | async-start | bytes 2228224 | tf_op jit(solution)/shard_map/all_gather | solution.py:119
  23.9 76.4 %all-gather.3.cloned.1.call-start = ((), (), s32[]{:S(2)}) async-start(), calls=%async_computation.4 | async-start | bytes 2228224 | tf_op jit(solution)/shard_map/all_gather | solution.py:118
  37.5 19.9 %all-to-all-start.1 = ((bf16[64,8,1024]{2,0,1:T(8,128)(2,1)}), bf16[64,8,1024]{2,0,1:T(8,128)(2,1)S(1)}, u32[]{:S(2)}, u32[]{:S(2)}) async-start(bf16[64,8,1024]{2,0,1:T(8,128)(2,1)} %bitcast.86), calls=%async_computation.1 | async-start | bytes 2097152 | tf_op jit(solution)/shard_map/all_to_all | solution.py:93
  107.2 6.3 %copy-start = (f32[512,512,8]{1,0,2:T(8,128)S(1)}, f32[512,512,8]{1,0,2:T(8,128)}, u32[]{:S(2)}) copy-start(f32[512,512,8]{1,0,2:T(8,128)} %get-tuple-element.318) | copy-start | bytes 25165828 | tf_op jit(solution)/shard_map/while
  122.4 6.3 %copy-start = (f32[512,512,8]{1,0,2:T(8,128)S(1)}, f32[512,512,8]{1,0,2:T(8,128)}, u32[]{:S(2)}) copy-start(f32[512,512,8]{1,0,2:T(8,128)} %get-tuple-element.318) | copy-start | bytes 25165828 | tf_op jit(solution)/shard_map/while
  137.5 6.3 %copy-start = (f32[512,512,8]{1,0,2:T(8,128)S(1)}, f32[512,512,8]{1,0,2:T(8,128)}, u32[]{:S(2)}) copy-start(f32[512,512,8]{1,0,2:T(8,128)} %get-tuple-element.318) | copy-start | bytes 25165828 | tf_op jit(solution)/shard_map/while
  152.6 6.3 %copy-start = (f32[512,512,8]{1,0,2:T(8,128)S(1)}, f32[512,512,8]{1,0,2:T(8,128)}, u32[]{:S(2)}) copy-start(f32[512,512,8]{1,0,2:T(8,128)} %get-tuple-element.318) | copy-start | bytes 25165828 | tf_op jit(solution)/shard_map/while
  167.7 6.3 %copy-start = (f32[512,512,8]{1,0,2:T(8,128)S(1)}, f32[512,512,8]{1,0,2:T(8,128)}, u32[]{:S(2)}) copy-start(f32[512,512,8]{1,0,2:T(8,128)} %get-tuple-element.318) | copy-start | bytes 25165828 | tf_op jit(solution)/shard_map/while
  182.9 6.3 %copy-start = (f32[512,512,8]{1,0,2:T(8,128)S(1)}, f32[512,512,8]{1,0,2:T(8,128)}, u32[]{:S(2)}) copy-start(f32[512,512,8]{1,0,2:T(8,128)} %get-tuple-element.318) | copy-start | bytes 25165828 | tf_op jit(solution)/shard_map/while
  198.0 6.3 %copy-start = (f32[512,512,8]{1,0,2:T(8,128)S(1)}, f32[512,512,8]{1,0,2:T(8,128)}, u32[]{:S(2)}) copy-start(f32[512,512,8]{1,0,2:T(8,128)} %get-tuple-element.318) | copy-start | bytes 25165828 | tf_op jit(solution)/shard_map/while
  213.1 6.3 %copy-start = (f32[512,512,8]{1,0,2:T(8,128)S(1)}, f32[512,512,8]{1,0,2:T(8,128)}, u32[]{:S(2)}) copy-start(f32[512,512,8]{1,0,2:T(8,128)} %get-tuple-element.318) | copy-start | bytes 25165828 | tf_op jit(solution)/shard_map/while
  228.2 6.3 %copy-start = (f32[512,512,8]{1,0,2:T(8,128)S(1)}, f32[512,512,8]{1,0,2:T(8,128)}, u32[]{:S(2)}) copy-start(f32[512,512,8]{1,0,2:T(8,128)} %get-tuple-element.318) | copy-start | bytes 25165828 | tf_op jit(solution)/shard_map/while
  243.4 6.3 %copy-start = (f32[512,512,8]{1,0,2:T(8,128)S(1)}, f32[512,512,8]{1,0,2:T(8,128)}, u32[]{:S(2)}) copy-start(f32[512,512,8]{1,0,2:T(8,128)} %get-tuple-element.318) | copy-start | bytes 25165828 | tf_op jit(solution)/shard_map/while
  258.5 6.3 %copy-start = (f32[512,512,8]{1,0,2:T(8,128)S(1)}, f32[512,512,8]{1,0,2:T(8,128)}, u32[]{:S(2)}) copy-start(f32[512,512,8]{1,0,2:T(8,128)} %get-tuple-element.318) | copy-start | bytes 25165828 | tf_op jit(solution)/shard_map/while
  273.6 6.3 %copy-start = (f32[512,512,8]{1,0,2:T(8,128)S(1)}, f32[512,512,8]{1,0,2:T(8,128)}, u32[]{:S(2)}) copy-start(f32[512,512,8]{1,0,2:T(8,128)} %get-tuple-element.318) | copy-start | bytes 25165828 | tf_op jit(solution)/shard_map/while
  288.7 6.3 %copy-start = (f32[512,512,8]{1,0,2:T(8,128)S(1)}, f32[512,512,8]{1,0,2:T(8,128)}, u32[]{:S(2)}) copy-start(f32[512,512,8]{1,0,2:T(8,128)} %get-tuple-element.318) | copy-start | bytes 25165828 | tf_op jit(solution)/shard_map/while
  303.9 6.3 %copy-start = (f32[512,512,8]{1,0,2:T(8,128)S(1)}, f32[512,512,8]{1,0,2:T(8,128)}, u32[]{:S(2)}) copy-start(f32[512,512,8]{1,0,2:T(8,128)} %get-tuple-element.318) | copy-start | bytes 25165828 | tf_op jit(solution)/shard_map/while
  319.0 6.3 %copy-start = (f32[512,512,8]{1,0,2:T(8,128)S(1)}, f32[512,512,8]{1,0,2:T(8,128)}, u32[]{:S(2)}) copy-start(f32[512,512,8]{1,0,2:T(8,128)} %get-tuple-element.318) | copy-start | bytes 25165828 | tf_op jit(solution)/shard_map/while
  334.1 6.3 %copy-start = (f32[512,512,8]{1,0,2:T(8,128)S(1)}, f32[512,512,8]{1,0,2:T(8,128)}, u32[]{:S(2)}) copy-start(f32[512,512,8]{1,0,2:T(8,128)} %get-tuple-element.318) | copy-start | bytes 25165828 | tf_op jit(solution)/shard_map/while
Sparse Core Ops, SparseCore 0:
  24.0 39.3 all-gather.4
  65.1 35.0 all-gather.2
where the time goes:
time: 376 us; the launch traced here: 375 us
  matrix products  190 us (51%)
  waiting for transfers between devices  58.7 us (16%)
  blocking collectives  50.2 us (13%)
  other arithmetic  42.6 us (11%)
  local copies, waits for them, and re-layouts  15.6 us (4%)
  between operations  13.6 us (4%)
    dot_general x16, matrix products, advance(): jnp.einsum('otzp,pth->otzh', weights.astype(jnp.bfloat16), block_of_value...  101 us
    dot_general x16, matrix products, advance(): jnp.einsum('foty,loy->fotl', query_group_count, block_of_keys, preferred_...  88.1 us
    all_gather x1, waiting for transfers between devices, on_device(): lax.all_gather(head_keys, 'blk', axis=0, tiled=True)  36.8 us
    reduce_sum x16, other arithmetic, advance(): new_sum = run_sum * factor + jnp.sum(weights, axis=-1)  27.7 us
    all_to_all x1, blocking collectives, on_device(): lax.all_to_all(finish(folded, rows_here), 'seq', split_axis=0, concat_axi...  23.5 us
    all_to_all x1, waiting for transfers between devices, on_device(): lax.all_to_all(queries, 'seq', split_axis=1, concat_axis=0, tiled=True)  16.2 us
    all_to_all x1, blocking collectives, on_device(): lax.all_to_all(rotated_values, 'seq', split_axis=1, concat_axis=0, tiled=...  15.7 us
    all_to_all x1, blocking collectives, on_device(): lax.all_to_all(rotated_keys, 'seq', split_axis=1, concat_axis=0, tiled=True)  11 us
  transfers between devices with their start and end apart: 3, of which 3 were waited for; matrix products, arithmetic and copies ran while one was open for 1% of the time, Pallas kernels for 0%

commit v1 on v0

v1 whole, which is shorter than its diff:
```python
import functools
import math

import jax
import jax.numpy as jnp
from jax import lax
from jax.experimental import pallas as pl
from jax.experimental.pallas import tpu as pltpu
from jax.sharding import Mesh, PartitionSpec as P

HEAD_DIM = 128
GROUP = 8
TOK = 64
AXES = ("y", "zh", "zl", "x", "core")
SIZES = (4, 2, 2, 4, 2)
HEADS_OVER = ("y", "zl")
COPIES_OVER = ("y", "zh", "zl")
CHUNK = GROUP * TOK
PAIR = 2 * CHUNK
STEP = 256
EARLY = 6
SCALE_LOG2 = HEAD_DIM ** (-0.5) * math.log2(math.e)
LOW, HIGH = 2.0**-60, 2.0**100
HIDDEN = -1e30
VMEM = pl.BlockSpec(memory_space=pltpu.VMEM)


def prepare_kernel(k_ref, v_ref, kv_ref):
    i = lax.broadcasted_iota(jnp.int32, (HEAD_DIM, HEAD_DIM), 0)
    j = lax.broadcasted_iota(jnp.int32, (HEAD_DIM, HEAD_DIM), 1)
    parity = i & j
    for shift in (4, 2, 1):
        parity = parity ^ (parity >> shift)
    matrix = (1 - 2 * (parity & 1)).astype(jnp.float32).astype(jnp.bfloat16)
    for part, ref in enumerate((k_ref, v_ref)):
        for h in range(ref.shape[1] // HEAD_DIM):
            turned = jnp.dot(
                ref[:, h * HEAD_DIM : (h + 1) * HEAD_DIM], matrix, preferred_element_type=jnp.float32
            ) * HEAD_DIM ** (-0.5)
            for zh in range(2):
                kv_ref[h // 2, zh, h % 2, part] = turned.astype(jnp.bfloat16)


def prepare(keys, values):
    return pl.pallas_call(
        prepare_kernel,
        out_shape=jax.ShapeDtypeStruct((4, 2, 2, 2, TOK, HEAD_DIM), jnp.bfloat16),
    )(keys, values)


class Tiles:
    def __init__(self, where_ref, first_slot, q_ref, acc_ref, block_refs, bias_ref):
        self.q, self.acc, self.blocks, self.bias = q_ref, acc_ref, block_refs, bias_ref
        self.zh = where_ref[0]
        token = lax.broadcasted_iota(jnp.int32, (TOK, TOK), 0)
        key = lax.broadcasted_iota(jnp.int32, (TOK, TOK), 1)
        for b in range(len(block_refs)):
            ahead = where_ref[2 + first_slot + b] - where_ref[1]
            bias_ref[:, b * TOK : (b + 1) * TOK] = jnp.where(ahead * TOK + key <= token, 0.0, HIDDEN)

    def load(self, part, quads):
        return jnp.concatenate([r[(*quad, part)] for quad in quads for r in self.blocks], axis=0)

    def scores(self, y, row, rows, quads, masked):
        x = (
            lax.dot_general(
                self.q[y, pl.ds(row, rows), :],
                self.load(0, quads),
                (((1,), (1,)), ((), ())),
                preferred_element_type=jnp.float32,
            )
            * SCALE_LOG2
        )
        if masked:
            seen = x.shape[1] - self.bias.shape[1]
            hidden = x[:, seen:] + jnp.concatenate([self.bias[...]] * (rows // TOK), axis=0)
            x = jnp.concatenate([x[:, :seen], hidden], axis=1) if seen else hidden
        return x

    def weigh(self, weights, quads):
        values = self.load(1, quads)
        return jnp.dot(
            weights.astype(jnp.bfloat16),
            jnp.concatenate([values, jnp.ones_like(values)], axis=1),
            preferred_element_type=jnp.float32,
        )

    def run(self, y, jobs, fresh):
        x = None
        for n, (row, quads, masked) in enumerate(jobs):
            if x is None:
                x = self.scores(y, row, STEP, quads, masked)
            weights = jnp.exp2(x)
            if n + 1 < len(jobs):
                x = self.scores(y, jobs[n + 1][0], STEP, *jobs[n + 1][1:])
            out = self.weigh(weights, quads)
            at = (y, pl.ds(row, STEP), slice(None))
            self.acc[at] = out if fresh else self.acc[at] + out

    def same_y(self, y, fresh):
        def jobs(others):
            listed = []
            for row in range(0, PAIR, STEP):
                own = [(y, self.zh, zl) for zl in range(row // CHUNK + 1)]
                listed.append((row, others + own, True))
            return listed

        @pl.when(self.zh == 1)
        def _():
            self.run(y, jobs([(y, 0, 0), (y, 0, 1)]), fresh)

        @pl.when(self.zh == 0)
        def _():
            self.run(y, jobs([]), fresh)

    def earlier_y(self, y):
        def one(key_y, carry):
            quads = [(key_y, zh, zl) for zh in range(2) for zl in range(2)]
            self.run(y, [(row, quads, False) for row in range(0, PAIR, STEP)], False)
            return carry

        lax.fori_loop(0, y, one, 0)


def first_kernel(*refs):
    where_ref, q_ref = refs[:2]
    block_refs = refs[2 : 2 + EARLY]
    acc_ref, bias_ref = refs[2 + EARLY :]
    tiles = Tiles(where_ref, 0, q_ref, acc_ref, block_refs, bias_ref)

    def pair(y, carry):
        tiles.same_y(y, True)
        tiles.earlier_y(y)
        return carry

    lax.fori_loop(0, 4, pair, 0)


def last_kernel(*refs):
    where_ref, q_ref, before_ref = refs[:3]
    block_refs = refs[3:11]
    o_ref, acc, bias, full_bias, top = refs[11:]
    tiles = Tiles(where_ref, EARLY, q_ref, acc, block_refs[EARLY:], bias)

    def pair(y, bad):
        acc[y] = before_ref[y]
        tiles.same_y(y, False)
        tiles.earlier_y(y)
        total = acc[y, :, HEAD_DIM:]
        o_ref[y] = (acc[y, :, :HEAD_DIM] / total).astype(jnp.bfloat16)
        fine = (total >= LOW) & (total <= HIGH)
        return jnp.maximum(bad, jnp.max(jnp.where(fine, 0.0, 1.0)))

    bad = lax.fori_loop(0, 4, pair, jnp.float32(0.0))

    @pl.when(bad > 0.0)
    def _():
        every = Tiles(where_ref, 0, q_ref, acc, block_refs, full_bias)

        def exact(y, zl, quad, first, masked):
            row = pl.multiple_of(zl * CHUNK, CHUNK)
            rows = pl.ds(row, CHUNK)
            x = every.scores(y, row, CHUNK, [quad], masked)
            high = jnp.max(x, axis=1, keepdims=True)
            if first:
                acc[y, rows, :] = every.weigh(jnp.exp2(x - high), [quad])
            else:
                before = top[:, :1]
                high = jnp.maximum(high, before)
                acc[y, rows, :] = acc[y, rows, :] * jnp.exp2(before - high) + every.weigh(
                    jnp.exp2(x - high), [quad]
                )
            top[...] = jnp.broadcast_to(high, top.shape)

        def exact_chunk(n, carry):
            y, zl = n // 2, n % 2
            exact(y, zl, (y, every.zh, zl), True, True)
            own = 4 * y + 2 * every.zh + zl

            def others(m, carry):
                exact(y, zl, (m // 4, m // 2 % 2, m % 2), False, False)
                return carry

            lax.fori_loop(0, own, others, 0)
            rows = pl.ds(pl.multiple_of(zl * CHUNK, CHUNK), CHUNK)
            o_ref[y, rows, :] = (acc[y, rows, :HEAD_DIM] / acc[y, rows, HEAD_DIM:]).astype(jnp.bfloat16)
            return carry

        lax.fori_loop(0, 8, exact_chunk, 0)


def cost(share):
    return pl.CostEstimate(
        flops=int(20e9 * share), bytes_accessed=6 * 2**20, transcendentals=int(2e7 * share)
    )


def attend_first(where, queries, blocks):
    return pl.pallas_call(
        first_kernel,
        out_shape=jax.ShapeDtypeStruct((4, PAIR, 2 * HEAD_DIM), jnp.float32),
        in_specs=[pl.BlockSpec(memory_space=pltpu.SMEM)] + [VMEM] * (1 + EARLY),
        out_specs=VMEM,
        scratch_shapes=[pltpu.VMEM((TOK, EARLY * TOK), jnp.float32)],
        compiler_params=pltpu.CompilerParams(vmem_limit_bytes=36 * 2**20),
        cost_estimate=cost(EARLY / 8),
    )(where, queries, *blocks)


def attend_last(where, queries, before, blocks):
    return pl.pallas_call(
        last_kernel,
        out_shape=jax.ShapeDtypeStruct((4, PAIR, HEAD_DIM), jnp.bfloat16),
        in_specs=[pl.BlockSpec(memory_space=pltpu.SMEM)] + [VMEM] * 10,
        out_specs=VMEM,
        scratch_shapes=[
            pltpu.VMEM((4, PAIR, 2 * HEAD_DIM), jnp.float32),
            pltpu.VMEM((TOK, (8 - EARLY) * TOK), jnp.float32),
            pltpu.VMEM((TOK, 8 * TOK), jnp.float32),
            pltpu.VMEM((CHUNK, HEAD_DIM), jnp.float32),
        ],
        compiler_params=pltpu.CompilerParams(vmem_limit_bytes=36 * 2**20),
        cost_estimate=cost(1 - EARLY / 8),
    )(where, queries, before, *blocks)


def fetch(array, axis, step):
    size = SIZES[AXES.index(axis)]
    return lax.ppermute(array, axis, [((n + step) % size, n) for n in range(size)])


def on_device(queries, keys, values):
    zh, x, core = (lax.axis_index(a) for a in ("zh", "x", "core"))
    kv = prepare(keys, values).reshape(16, 2, TOK, HEAD_DIM)
    own = lax.all_to_all(kv, COPIES_OVER, split_axis=0, concat_axis=0, tiled=True)
    own = own.reshape(4, 2, 2, 2, TOK, HEAD_DIM)
    q = queries.reshape(TOK, 8 * GROUP, HEAD_DIM).transpose(1, 0, 2).reshape(8, CHUNK, HEAD_DIM)
    q, _ = lax.optimization_barrier((q, own))
    q = lax.all_to_all(q, HEADS_OVER, split_axis=0, concat_axis=0, tiled=True)
    q = q.reshape(4, PAIR, HEAD_DIM)
    blocks, slots = [], []
    for step in (0, 1, 3, 2):
        block = fetch(own, "x", step) if step else own
        blocks += [block, fetch(block, "core", 1)]
        slots += [(x + step) % 4 * 2 + core, (x + step) % 4 * 2 + 1 - core]
    where = jnp.stack([zh, x * 2 + core] + slots).astype(jnp.int32)
    acc = attend_first(where, q, blocks[:EARLY])
    out = attend_last(where, q, acc, blocks).reshape(8, CHUNK, HEAD_DIM)
    out = lax.all_to_all(out, HEADS_OVER, split_axis=0, concat_axis=0, tiled=True)
    return out.reshape(8 * GROUP, TOK, HEAD_DIM).transpose(1, 0, 2).reshape(queries.shape)


def solution(mesh):
    fine = Mesh(mesh.devices.reshape(SIZES), AXES)
    spec = P(AXES, None)
    return jax.shard_map(
        on_device, mesh=fine, in_specs=(spec,) * 3, out_specs=spec, check_vma=False
    )
```

time: 376 us -> 181 us (0.48)
  the two profiles are of different devices: /device:TPU:0 before, /device:TPU:71 now
where the time goes in v1:
time: 181 us
  Pallas kernels  121 us (67%)
  blocking collectives  28.2 us (16%)
  starting transfers between devices  23.9 us (13%)
  local copies, waits for them, and re-layouts  5.61 us (3%)
    pallas_call x1, Pallas kernels, attend_last(): pl.pallas_call(last_kernel, out_shape=jax.ShapeDtypeStruct((4, PAIR, HEAD...  101 us
    ppermute x7, starting transfers between devices, fetch(): lax.ppermute(array, axis, [((n + step) % size, n) for n in range(size)])  20.3 us
    pallas_call x1, Pallas kernels, attend_first(): pl.pallas_call(first_kernel, out_shape=jax.ShapeDtypeStruct((4, PAIR, 2 *...  18.8 us
    all_to_all x1, blocking collectives, on_device(): lax.all_to_all(kv, COPIES_OVER, split_axis=0, concat_axis=0, tiled=True)  15.5 us
    all_to_all x1, blocking collectives, on_device(): lax.all_to_all(out, HEADS_OVER, split_axis=0, concat_axis=0, tiled=True)  12.7 us
  transfers between devices with their start and end apart: 8, of which 1 were waited for; matrix products, arithmetic and copies ran while one was open for 2% of the time, Pallas kernels for 10%

profile of v1, /device:TPU:71, one launch (start us, length us, event | category | flops | bytes accessed | tf_op | source)
XLA Modules:
  0.0 180.7 jit_solution(9064469479574627547)
XLA Ops:
  0.0 2.1 %shard_map.37 = bf16[4,2,2,2,64,128]{5,4,3,2,1,0:T(8,128)(2,1)} custom-call(bf16[64,1024]{1,0:T(8,128)(2,1)} %k_ref.1, bf16[64,1024]{1,0:T(8,128)(2,1)} %v_ref.1), custom_call_target="tpu_custom_call" | custom-call | tf_op jit(solution)/shard_map/pallas_call | solution.py:45
  2.1 15.5 %all_to_all.15 = bf16[16,2,64,128]{3,2,1,0:T(8,128)(2,1)S(1)} all-to-all(bf16[16,2,64,128]{3,2,1,0:T(8,128)(2,1)} %bitcast.38), channel_id=1, replica_groups=mesh['y'=4,'zh'=2,'zl'=2,'x'=4,'core'=2] {'y','zh','zl'}, dimensions={0} | all-to-all | bytes 1048576 | tf_op jit(solution)/shard_map/all_to_all | solution.py:235
  17.6 0.2 collective-permute-start.3
  17.8 1.3 collective-permute-start.1
  19.0 1.5 copy.6
  20.5 1.7 copy.4
  22.2 3.6 %all-to-all-start.1 = ((bf16[8,512,128]{2,1,0:T(8,128)(2,1)}), bf16[8,512,128]{2,1,0:T(8,128)(2,1)S(1)}, u32[]{:S(2)}, u32[]{:S(2)}) async-start(bf16[8,512,128]{2,1,0:T(8,128)(2,1)} %bitcast.34), calls=%async_computation.1 | async-start | bytes 2097152 | tf_op jit(solution)/shard_map/all_to_all | solution.py:239
  25.8 1.2 collective-permute-start.5
  27.0 2.8 %collective-permute-start = (bf16[4,2,2,2,64,128]{5,4,3,2,1,0:T(8,128)(2,1)S(1)}, bf16[4,2,2,2,64,128]{5,4,3,2,1,0:T(8,128)(2,1)}, u32[]{:S(2)}, u32[]{:S(2)}) collective-permute-start(bf16[4,2,2,2,64,128]{5,4,3,2,1,0:T(8,128)(2,1)S(1)} %bitcast.31), channel_id=1, source_target_pairs={{1,0},{0,1},{3,2},{2,3},{5,4},{4,5},{7,6},{6,7},{9,8},{8,9},{11,10... | collective-permute-start | bytes 1572872 | tf_op jit(solution)/shard_map/ppermute | solution.py:229
  29.7 0.0 collective-permute-done.3.refs_6_.refs_7_
  29.7 4.5 %collective-permute-start.4 = (bf16[4,2,2,2,64,128]{5,4,3,2,1,0:T(8,128)(2,1)S(1)}, bf16[4,2,2,2,64,128]{5,4,3,2,1,0:T(8,128)(2,1)}, u32[]{:S(2)}, u32[]{:S(2)}) collective-permute-start(bf16[4,2,2,2,64,128]{5,4,3,2,1,0:T(8,128)(2,1)S(1)} %collective-permute-done.3.refs_6_.refs_7_), channel_id=1, source_target_pairs={{1,0},{0,1},{3,2},{2,3},{5,4},{4,5},{7,6},{6,7},{9,8},{8,9},{11,10... | collective-permute-start | bytes 1572872 | tf_op jit(solution)/shard_map/ppermute | solution.py:229
  34.3 0.0 collective-permute-done.1.refs_4_.refs_5_
  34.3 10.3 %collective-permute-start.2 = (bf16[4,2,2,2,64,128]{5,4,3,2,1,0:T(8,128)(2,1)S(1)}, bf16[4,2,2,2,64,128]{5,4,3,2,1,0:T(8,128)(2,1)}, u32[]{:S(2)}, u32[]{:S(2)}) collective-permute-start(bf16[4,2,2,2,64,128]{5,4,3,2,1,0:T(8,128)(2,1)S(1)} %collective-permute-done.1.refs_4_.refs_5_), channel_id=1, source_target_pairs={{1,0},{0,1},{3,2},{2,3},{5,4},{4,5},{7,6},{6,7},{9,8},{8,9},{11,10... | collective-permute-start | bytes 1572872 | tf_op jit(solution)/shard_map/ppermute | solution.py:229
  44.6 0.1 stack.43.refs_0_
  44.6 0.0 collective-permute-done.5.refs_9_
  44.6 0.1 collective-permute-start.6
  44.7 0.0 collective-permute-done.refs_3_.refs_4_
  44.8 0.0 all-to-all-done.1
  44.8 1.5 collective-permute-done.2.refs_5_.refs_6_
  46.2 18.8 %shard_map.38.refs_2_ = f32[4,1024,256]{2,1,0:T(8,128)S(1)} custom-call(s32[10]{0:T(128)S(1)} %stack.43.refs_0_, bf16[4,1024,128]{2,1,0:T(8,128)(2,1)S(1)} %bitcast.25, bf16[4,2,2,2,64,128]{5,4,3,2,1,0:T(8,128)(2,1)S(1)} %bitcast.32, bf16[4,2,2,2,64,128]{5,4,3,2,1,0:T(8,128)(2,1)} %collective-permute-done.refs_3_.refs_4_, ...), custom_call_target="tpu_custom_call" | custom-call | flops 15000000512 | bytes 6291456 | tf_op jit(solution)/shard_map/pallas_call | solution.py:199
  65.0 100.5 %shard_map.39 = bf16[4,1024,128]{2,1,0:T(8,128)(2,1)S(1)} custom-call(s32[10]{0:T(128)S(1)} %stack.43.refs_0_, bf16[4,1024,128]{2,1,0:T(8,128)(2,1)S(1)} %bitcast.26, f32[4,1024,256]{2,1,0:T(8,128)S(1)} %shard_map.38.refs_2_, bf16[4,2,2,2,64,128]{5,4,3,2,1,0:T(8,128)(2,1)S(1)} %bitcast.33, ...), custom_call_target="tpu_custom_call" | custom-call | flops 5000000000 | bytes 6291456 | tf_op jit(solution)/shard_map/pallas_call | solution.py:211
  165.6 12.7 %all_to_all.16 = bf16[8,512,128]{2,1,0:T(8,128)(2,1)S(1)} all-to-all(bf16[8,512,128]{2,1,0:T(8,128)(2,1)S(1)} %bitcast.27), channel_id=1, replica_groups=mesh['y'=4,'zh'=2,'zl'=2,'x'=4,'core'=2] {'y','zl'}, dimensions={0} | all-to-all | bytes 2097152 | tf_op jit(solution)/shard_map/all_to_all | solution.py:249
  178.3 0.7 copy.5
  179.0 1.7 copy.9
  (2 shorter events, 0.0 us)
Async XLA Ops:
  17.6 12.2 %collective-permute-start.3 = (bf16[4,2,2,2,64,128]{5,4,3,2,1,0:T(8,128)(2,1)S(1)}, bf16[4,2,2,2,64,128]{5,4,3,2,1,0:T(8,128)(2,1)S(1)}, u32[]{:S(2)}, u32[]{:S(2)}) collective-permute-start(bf16[4,2,2,2,64,128]{5,4,3,2,1,0:T(8,128)(2,1)S(1)} %bitcast.28), channel_id=1, source_target_pairs={{6,0},{0,2},{2,4},{4,6},{7,1},{1,3},{3,5},{5,7},{14,8},{8,10},{10,... | collective-permute-start | bytes 1572872 | tf_op jit(solution)/shard_map/ppermute | solution.py:229
  17.8 16.5 %collective-permute-start.1 = (bf16[4,2,2,2,64,128]{5,4,3,2,1,0:T(8,128)(2,1)S(1)}, bf16[4,2,2,2,64,128]{5,4,3,2,1,0:T(8,128)(2,1)S(1)}, u32[]{:S(2)}, u32[]{:S(2)}) collective-permute-start(bf16[4,2,2,2,64,128]{5,4,3,2,1,0:T(8,128)(2,1)S(1)} %bitcast.29), channel_id=1, source_target_pairs={{2,0},{4,2},{6,4},{0,6},{3,1},{5,3},{7,5},{1,7},{10,8},{12,10},{14... | collective-permute-start | bytes 1572872 | tf_op jit(solution)/shard_map/ppermute | solution.py:229
  22.2 22.6 %all-to-all-start.1 = ((bf16[8,512,128]{2,1,0:T(8,128)(2,1)}), bf16[8,512,128]{2,1,0:T(8,128)(2,1)S(1)}, u32[]{:S(2)}, u32[]{:S(2)}) async-start(bf16[8,512,128]{2,1,0:T(8,128)(2,1)} %bitcast.34), calls=%async_computation.1 | async-start | bytes 2097152 | tf_op jit(solution)/shard_map/all_to_all | solution.py:239
  25.8 18.9 %collective-permute-start.5 = (bf16[4,2,2,2,64,128]{5,4,3,2,1,0:T(8,128)(2,1)S(1)}, bf16[4,2,2,2,64,128]{5,4,3,2,1,0:T(8,128)(2,1)S(1)}, u32[]{:S(2)}, u32[]{:S(2)}) collective-permute-start(bf16[4,2,2,2,64,128]{5,4,3,2,1,0:T(8,128)(2,1)S(1)} %bitcast.30), channel_id=1, source_target_pairs={{4,0},{6,2},{0,4},{2,6},{5,1},{7,3},{1,5},{3,7},{12,8},{14,10},{8,... | collective-permute-start | bytes 1572872 | tf_op jit(solution)/shard_map/ppermute | solution.py:229
  27.0 17.8 %collective-permute-start = (bf16[4,2,2,2,64,128]{5,4,3,2,1,0:T(8,128)(2,1)S(1)}, bf16[4,2,2,2,64,128]{5,4,3,2,1,0:T(8,128)(2,1)}, u32[]{:S(2)}, u32[]{:S(2)}) collective-permute-start(bf16[4,2,2,2,64,128]{5,4,3,2,1,0:T(8,128)(2,1)S(1)} %bitcast.31), channel_id=1, source_target_pairs={{1,0},{0,1},{3,2},{2,3},{5,4},{4,5},{7,6},{6,7},{9,8},{8,9},{11,10... | collective-permute-start | bytes 1572872 | tf_op jit(solution)/shard_map/ppermute | solution.py:229
  29.7 15.0 %collective-permute-start.4 = (bf16[4,2,2,2,64,128]{5,4,3,2,1,0:T(8,128)(2,1)S(1)}, bf16[4,2,2,2,64,128]{5,4,3,2,1,0:T(8,128)(2,1)}, u32[]{:S(2)}, u32[]{:S(2)}) collective-permute-start(bf16[4,2,2,2,64,128]{5,4,3,2,1,0:T(8,128)(2,1)S(1)} %collective-permute-done.3.refs_6_.refs_7_), channel_id=1, source_target_pairs={{1,0},{0,1},{3,2},{2,3},{5,4},{4,5},{7,6},{6,7},{9,8},{8,9},{11,10... | collective-permute-start | bytes 1572872 | tf_op jit(solution)/shard_map/ppermute | solution.py:229
  34.3 11.9 %collective-permute-start.2 = (bf16[4,2,2,2,64,128]{5,4,3,2,1,0:T(8,128)(2,1)S(1)}, bf16[4,2,2,2,64,128]{5,4,3,2,1,0:T(8,128)(2,1)}, u32[]{:S(2)}, u32[]{:S(2)}) collective-permute-start(bf16[4,2,2,2,64,128]{5,4,3,2,1,0:T(8,128)(2,1)S(1)} %collective-permute-done.1.refs_4_.refs_5_), channel_id=1, source_target_pairs={{1,0},{0,1},{3,2},{2,3},{5,4},{4,5},{7,6},{6,7},{9,8},{8,9},{11,10... | collective-permute-start | bytes 1572872 | tf_op jit(solution)/shard_map/ppermute | solution.py:229
  44.6 20.4 %collective-permute-start.6 = (bf16[4,2,2,2,64,128]{5,4,3,2,1,0:T(8,128)(2,1)S(1)}, bf16[4,2,2,2,64,128]{5,4,3,2,1,0:T(8,128)(2,1)}, u32[]{:S(2)}, u32[]{:S(2)}) collective-permute-start(bf16[4,2,2,2,64,128]{5,4,3,2,1,0:T(8,128)(2,1)S(1)} %collective-permute-done.5.refs_9_), channel_id=1, source_target_pairs={{1,0},{0,1},{3,2},{2,3},{5,4},{4,5},{7,6},{6,7},{9,8},{8,9},{11,10... | collective-permute-start | bytes 1572872 | tf_op jit(solution)/shard_map/ppermute | solution.py:229

commit v2 on v1

v2 whole, which is shorter than its diff:
```python
import math

import jax
import jax.numpy as jnp
from jax import lax
from jax.experimental import pallas as pl
from jax.experimental.pallas import tpu as pltpu
from jax.sharding import Mesh, PartitionSpec as P

HEAD_DIM = 128
GROUP = 8
TOK = 64
SIZES = {"yz": 16, "xc": 8}
TRADERS = [[4 * y + z for y in range(4) for z in zs] for zs in ((0, 3), (1, 2))]
CHUNK = GROUP * TOK
PAIR = 2 * CHUNK
STEP = 256
SCALE_LOG2 = HEAD_DIM ** (-0.5) * math.log2(math.e)
LOW, HIGH = 2.0**-60, 2.0**100
HIDDEN = -1e30
VMEM = pl.BlockSpec(memory_space=pltpu.VMEM)


def prepare_kernel(k_ref, v_ref, kv_ref):
    i = lax.broadcasted_iota(jnp.int32, (HEAD_DIM, HEAD_DIM), 0)
    j = lax.broadcasted_iota(jnp.int32, (HEAD_DIM, HEAD_DIM), 1)
    parity = i & j
    for shift in (4, 2, 1):
        parity = parity ^ (parity >> shift)
    matrix = (1 - 2 * (parity & 1)).astype(jnp.float32).astype(jnp.bfloat16)
    heads = k_ref.shape[1] // HEAD_DIM
    for part, ref in enumerate((k_ref, v_ref)):
        rows = jnp.concatenate([ref[:, h * HEAD_DIM : (h + 1) * HEAD_DIM] for h in range(heads)], axis=0)
        turned = jnp.dot(rows, matrix, preferred_element_type=jnp.float32) * HEAD_DIM ** (-0.5)
        turned = turned.astype(jnp.bfloat16)
        for h in range(heads):
            for n in range(2):
                kv_ref[2 * h + n, part] = turned[h * TOK : (h + 1) * TOK]


def prepare(keys, values):
    return pl.pallas_call(
        prepare_kernel,
        out_shape=jax.ShapeDtypeStruct((16, 2, TOK, HEAD_DIM), jnp.bfloat16),
    )(keys, values)


def by_head_kernel(q_ref, o_ref):
    for h in range(o_ref.shape[0]):
        o_ref[h] = q_ref[:, h * HEAD_DIM : (h + 1) * HEAD_DIM]


def by_head(queries):
    heads = queries.shape[1] // HEAD_DIM
    return pl.pallas_call(
        by_head_kernel,
        out_shape=jax.ShapeDtypeStruct((heads, TOK, HEAD_DIM), jnp.bfloat16),
    )(queries)


def after_kernel(array_ref, token_ref, o_ref):
    del array_ref, token_ref, o_ref


def after(array, token):
    return pl.pallas_call(
        after_kernel,
        out_shape=jax.ShapeDtypeStruct(array.shape, array.dtype),
        in_specs=[pl.BlockSpec(memory_space=pl.ANY)] * 2,
        out_specs=pl.BlockSpec(memory_space=pl.ANY),
        input_output_aliases={0: 0},
        cost_estimate=pl.CostEstimate(flops=5 * 10**9, bytes_accessed=0, transcendentals=0),
    )(array, token)


def attend_kernel(*refs):
    where_ref, q_ref = refs[:2]
    block_refs = refs[2:10]
    o_ref, acc, bias, top = refs[10:]
    inner = where_ref[0]
    token = lax.broadcasted_iota(jnp.int32, (TOK, TOK), 0)
    key = lax.broadcasted_iota(jnp.int32, (TOK, TOK), 1)
    for b in range(8):
        ahead = where_ref[2 + b] - where_ref[1]
        bias[:, b * TOK : (b + 1) * TOK] = jnp.where(ahead * TOK + key <= token, 0.0, HIDDEN)

    def load(part, quads):
        return jnp.concatenate([r[(*quad, part)] for quad in quads for r in block_refs], axis=0)

    def scores(y, row, rows, quads, masked):
        x = (
            lax.dot_general(
                q_ref[y, pl.ds(row, rows), :],
                load(0, quads),
                (((1,), (1,)), ((), ())),
                preferred_element_type=jnp.float32,
            )
            * SCALE_LOG2
        )
        if masked:
            seen = x.shape[1] - bias.shape[1]
            hidden = x[:, seen:] + jnp.concatenate([bias[...]] * (rows // TOK), axis=0)
            x = jnp.concatenate([x[:, :seen], hidden], axis=1) if seen else hidden
        return x

    def weigh(weights, quads):
        values = load(1, quads)
        return jnp.dot(
            weights.astype(jnp.bfloat16),
            jnp.concatenate([values, jnp.ones_like(values)], axis=1),
            preferred_element_type=jnp.float32,
        )

    def run(y, jobs, fresh):
        x = scores(y, jobs[0][0], STEP, *jobs[0][1:])
        for n, (row, quads, _) in enumerate(jobs):
            weights = jnp.exp2(x)
            if n + 1 < len(jobs):
                x = scores(y, jobs[n + 1][0], STEP, *jobs[n + 1][1:])
            out = weigh(weights, quads)
            at = pl.ds(row, STEP)
            acc[at, :] = out if fresh else acc[at, :] + out

    def same_y(y, zs):
        jobs = [
            (row, [(y, z) for z in range(zs[row // CHUNK] + 1)], True) for row in range(0, PAIR, STEP)
        ]
        run(y, jobs, True)

    def store(y, m):
        rows = slice(m * CHUNK, (m + 1) * CHUNK)
        out = (acc[rows, :HEAD_DIM] / acc[rows, HEAD_DIM:]).astype(jnp.bfloat16)
        for h in range(GROUP):
            o_ref[2 * y + m, :, h * HEAD_DIM : (h + 1) * HEAD_DIM] = out[h * TOK : (h + 1) * TOK]

    def pair(y, bad):
        pl.when(inner == 0)(lambda: same_y(y, (0, 3)))
        pl.when(inner == 1)(lambda: same_y(y, (1, 2)))

        def earlier(key_y, carry):
            quads = [(key_y, z) for z in range(4)]
            run(y, [(row, quads, False) for row in range(0, PAIR, STEP)], False)
            return carry

        lax.fori_loop(0, y, earlier, 0)
        total = acc[:, HEAD_DIM:]
        for m in range(2):
            store(y, m)
        fine = (total >= LOW) & (total <= HIGH)
        return jnp.maximum(bad, jnp.max(jnp.where(fine, 0.0, 1.0)))

    bad = lax.fori_loop(0, 4, pair, jnp.float32(0.0))

    @pl.when(bad > 0.0)
    def _():
        def exact(y, m, quad, first):
            row = pl.multiple_of(m * CHUNK, CHUNK)
            rows = pl.ds(row, CHUNK)
            x = scores(y, row, CHUNK, [quad], first)
            high = jnp.max(x, axis=1, keepdims=True)
            if first:
                acc[rows, :] = weigh(jnp.exp2(x - high), [quad])
            else:
                before = top[:, :1]
                high = jnp.maximum(high, before)
                acc[rows, :] = acc[rows, :] * jnp.exp2(before - high) + weigh(jnp.exp2(x - high), [quad])
            top[...] = jnp.broadcast_to(high, top.shape)

        def exact_chunk(n, m):
            z = inner + m * (3 - 2 * inner)
            exact(n, m, (n, z), True)

            def others(k, carry):
                exact(n, m, (k // 4, k % 4), False)
                return carry

            lax.fori_loop(0, 4 * n + z, others, 0)
            store(n, m)

        def exact_pair(y, carry):
            for m in range(2):
                exact_chunk(y, m)
            return carry

        lax.fori_loop(0, 4, exact_pair, 0)


def attend(where, queries, blocks):
    return pl.pallas_call(
        attend_kernel,
        out_shape=jax.ShapeDtypeStruct((8, TOK, GROUP * HEAD_DIM), jnp.bfloat16),
        in_specs=[pl.BlockSpec(memory_space=pltpu.SMEM)] + [VMEM] * 9,
        out_specs=VMEM,
        scratch_shapes=[
            pltpu.VMEM((PAIR, 2 * HEAD_DIM), jnp.float32),
            pltpu.VMEM((TOK, 8 * TOK), jnp.float32),
            pltpu.VMEM((CHUNK, HEAD_DIM), jnp.float32),
        ],
        compiler_params=pltpu.CompilerParams(vmem_limit_bytes=20 * 2**20),
        cost_estimate=pl.CostEstimate(flops=2 * 10**10, bytes_accessed=6 * 2**20, transcendentals=2 * 10**7),
    )(where, queries, *blocks)


def around(array, step):
    return lax.ppermute(array, "xc", [((n + 2 * step) % 8, n) for n in range(8)])


def across(array):
    return lax.ppermute(array, "yz", [(n ^ 1, n) for n in range(16)])


def swap(array):
    return lax.ppermute(array, "xc", [(n ^ 1, n) for n in range(8)])


def trade(array):
    return lax.all_to_all(array, "yz", split_axis=0, concat_axis=0, tiled=True, axis_index_groups=TRADERS)


def on_device(queries, keys, values):
    z, xc = lax.axis_index("yz") % 4, lax.axis_index("xc")
    kv = prepare(keys, values)
    own = lax.all_to_all(kv, "yz", split_axis=0, concat_axis=0, tiled=True)
    q = by_head(queries).reshape(8, CHUNK, HEAD_DIM)
    q, own = lax.optimization_barrier((q, own))
    own = own.reshape(4, 4, 2, TOK, HEAD_DIM)
    other = swap(own)
    q = trade(after(q, own)).reshape(4, PAIR, HEAD_DIM)
    inner = (z == 1) | (z == 2)
    half = around(jnp.where(inner, own[2:], own[:2]), 2)
    rest = across(half)
    far = jnp.concatenate([jnp.where(inner, rest, half), jnp.where(inner, half, rest)], axis=0)
    blocks, slots = [own, other], [xc, xc ^ 1]
    for step, block in ((1, around(own, 1)), (3, around(own, 3)), (2, far)):
        blocks += [block, swap(block)]
        slots += [(xc + 2 * step) % 8, (xc + 2 * step) % 8 ^ 1]
    where = jnp.stack([jnp.where(inner, 1, 0), xc] + slots).astype(jnp.int32)
    out = trade(attend(where, q, blocks))
    return out.transpose(1, 0, 2).reshape(queries.shape)


def solution(mesh):
    fine = Mesh(mesh.devices.reshape(tuple(SIZES.values())), tuple(SIZES))
    spec = P(tuple(SIZES), None)
    return jax.shard_map(
        on_device, mesh=fine, in_specs=(spec,) * 3, out_specs=spec, check_vma=False
    )
```

time: 181 us -> 170 us (0.939)
  the two profiles are of different devices: /device:TPU:71 before, /device:TPU:0 now
where the time goes in v2:
time: 170 us
  Pallas kernels  108 us (64%)
  waiting for transfers between devices  24.5 us (14%)
  starting transfers between devices  19.3 us (11%)
  blocking collectives  16 us (9%)
    pallas_call x1, Pallas kernels, attend(): pl.pallas_call(attend_kernel, out_shape=jax.ShapeDtypeStruct((8, TOK, GRO...  103 us
    all_to_all x1, blocking collectives, trade(): lax.all_to_all(array, 'yz', split_axis=0, concat_axis=0, tiled=True, axis...  16 us
    all_to_all x1, waiting for transfers between devices, on_device(): own = lax.all_to_all(kv, 'yz', split_axis=0, concat_axis=0, tiled=True)  9.15 us
    all_to_all x1, starting transfers between devices, on_device(): own = lax.all_to_all(kv, 'yz', split_axis=0, concat_axis=0, tiled=True)  8.18 us
    all_to_all x1, waiting for transfers between devices, trade(): lax.all_to_all(array, 'yz', split_axis=0, concat_axis=0, tiled=True, axis...  6.65 us
    ppermute x3, waiting for transfers between devices, around(): lax.ppermute(array, 'xc', [((n + 2 * step) % 8, n) for n in range(8)])  6.57 us
    ppermute x3, starting transfers between devices, around(): lax.ppermute(array, 'xc', [((n + 2 * step) % 8, n) for n in range(8)])  6.34 us
    all_to_all x1, starting transfers between devices, trade(): lax.all_to_all(array, 'yz', split_axis=0, concat_axis=0, tiled=True, axis...  3.56 us
  transfers between devices with their start and end apart: 10, of which 6 were waited for; matrix products, arithmetic and copies ran while one was open for 0% of the time, Pallas kernels for 1%

profile of v2, /device:TPU:0, one launch (start us, length us, event | category | flops | bytes accessed | tf_op | source)
XLA Modules:
  0.0 169.8 jit_solution(9984912333394693702)
XLA Ops:
  0.0 2.0 %shard_map.38 = bf16[16,2,64,128]{3,2,1,0:T(8,128)(2,1)} custom-call(bf16[64,1024]{1,0:T(8,128)(2,1)} %k_ref.1, bf16[64,1024]{1,0:T(8,128)(2,1)} %v_ref.1), custom_call_target="tpu_custom_call" | custom-call | tf_op jit(solution)/shard_map/pallas_call | solution.py:42
  2.0 8.2 %all-to-all-start = ((bf16[16,2,64,128]{3,2,1,0:T(8,128)(2,1)}), bf16[16,2,64,128]{3,2,1,0:T(8,128)(2,1)}, u32[]{:S(2)}, u32[]{:S(2)}) async-start(bf16[16,2,64,128]{3,2,1,0:T(8,128)(2,1)} %shard_map.38), calls=%async_computation | async-start | bytes 1048576 | tf_op jit(solution)/shard_map/all_to_all | solution.py:223
  10.2 2.4 %shard_map.37 = bf16[64,64,128]{2,1,0:T(8,128)(2,1)} custom-call(bf16[64,8192]{1,0:T(8,128)(2,1)} %q_ref.1), custom_call_target="tpu_custom_call" | custom-call | tf_op jit(solution)/shard_map/pallas_call | solution.py:55
  12.6 9.1 %all-to-all-done = bf16[16,2,64,128]{3,2,1,0:T(8,128)(2,1)} async-done(((bf16[16,2,64,128]{3,2,1,0:T(8,128)(2,1)}), bf16[16,2,64,128]{3,2,1,0:T(8,128)(2,1)}, u32[]{:S(2)}, u32[]{:S(2)}) %all-to-all-start) | async-done | bytes 524320 | tf_op jit(solution)/shard_map/all_to_all | solution.py:223
  21.7 1.1 slice_select_fusion
  22.8 3.1 %collective-permute-start.5 = (bf16[2,4,2,64,128]{4,3,2,1,0:T(8,128)(2,1)S(1)}, bf16[2,4,2,64,128]{4,3,2,1,0:T(8,128)(2,1)S(1)}, u32[]{:S(2)}, u32[]{:S(2)}) collective-permute-start(bf16[2,4,2,64,128]{4,3,2,1,0:T(8,128)(2,1)S(1)} %bitcast.19), channel_id=1, source_target_pairs={{4,0},{5,1},{6,2},{7,3},{0,4},{1,5},{2,6},{3,7},{12,8},{13,9},{14,... | collective-permute-start | bytes 786440 | tf_op jit(solution)/shard_map/ppermute | solution.py:205
  25.9 0.6 collective-permute-start.3
  26.5 2.6 %collective-permute-start.1 = (bf16[4,4,2,64,128]{4,3,2,1,0:T(8,128)(2,1)}, bf16[4,4,2,64,128]{4,3,2,1,0:T(8,128)(2,1)S(1)}, u32[]{:S(2)}, u32[]{:S(2)}) collective-permute-start(bf16[4,4,2,64,128]{4,3,2,1,0:T(8,128)(2,1)} %bitcast.10.token_ref.refs_2_), channel_id=1, source_target_pairs={{2,0},{3,1},{4,2},{5,3},{6,4},{7,5},{0,6},{1,7},{10,8},{11,9},{12,... | collective-permute-start | bytes 1572872 | tf_op jit(solution)/shard_map/ppermute | solution.py:205
  29.1 4.5 %collective-permute-done.5 = bf16[2,4,2,64,128]{4,3,2,1,0:T(8,128)(2,1)S(1)} collective-permute-done((bf16[2,4,2,64,128]{4,3,2,1,0:T(8,128)(2,1)S(1)}, bf16[2,4,2,64,128]{4,3,2,1,0:T(8,128)(2,1)S(1)}, u32[]{:S(2)}, u32[]{:S(2)}) %collective-permute-start.5) | collective-permute-done | bytes 262176 | tf_op jit(solution)/shard_map/ppermute | solution.py:205
  33.6 0.6 collective-permute-start.6
  34.2 3.6 %all-to-all-start.1 = ((bf16[8,512,128]{2,1,0:T(8,128)(2,1)}), bf16[8,512,128]{2,1,0:T(8,128)(2,1)S(1)}, u32[]{:S(2)}, u32[]{:S(2)}) async-start(bf16[8,512,128]{2,1,0:T(8,128)(2,1)} %shard_map.39), calls=%async_computation.1 | async-start | bytes 2097152 | tf_op jit(solution)/shard_map/all_to_all | solution.py:217
  37.8 0.1 collective-permute-start
  37.8 2.1 %collective-permute-done.6 = bf16[2,4,2,64,128]{4,3,2,1,0:T(8,128)(2,1)S(1)} collective-permute-done((bf16[2,4,2,64,128]{4,3,2,1,0:T(8,128)(2,1)S(1)}, bf16[2,4,2,64,128]{4,3,2,1,0:T(8,128)(2,1)S(1)}, u32[]{:S(2)}, u32[]{:S(2)}) %collective-permute-start.6) | collective-permute-done | bytes 262176 | tf_op jit(solution)/shard_map/ppermute | solution.py:209
  40.1 0.1 collective-permute-start.7
  40.2 2.0 %collective-permute-done.3.refs_6_ = bf16[4,4,2,64,128]{4,3,2,1,0:T(8,128)(2,1)S(1)} collective-permute-done((bf16[4,4,2,64,128]{4,3,2,1,0:T(8,128)(2,1)}, bf16[4,4,2,64,128]{4,3,2,1,0:T(8,128)(2,1)S(1)}, u32[]{:S(2)}, u32[]{:S(2)}) %collective-permute-start.3) | collective-permute-done | bytes 524320 | tf_op jit(solution)/shard_map/ppermute | solution.py:205
  42.2 0.0 collective-permute-start.4
  42.2 0.1 collective-permute-done.1.refs_4_
  42.3 0.4 collective-permute-start.2
  42.7 0.1 stack.40.refs_0_
  42.8 0.0 collective-permute-done.refs_3_
  42.8 6.7 %all-to-all-done.1 = bf16[8,512,128]{2,1,0:T(8,128)(2,1)S(1)} async-done(((bf16[8,512,128]{2,1,0:T(8,128)(2,1)}), bf16[8,512,128]{2,1,0:T(8,128)(2,1)S(1)}, u32[]{:S(2)}, u32[]{:S(2)}) %all-to-all-start.1) | async-done | bytes 1048608 | tf_op jit(solution)/shard_map/all_to_all | solution.py:217
  49.5 103.2 %shard_map.40 = bf16[8,64,1024]{2,1,0:T(8,128)(2,1)S(1)} custom-call(s32[10]{0:T(128)S(1)} %stack.40.refs_0_, bf16[4,1024,128]{2,1,0:T(8,128)(2,1)S(1)} %bitcast.16, bf16[4,4,2,64,128]{4,3,2,1,0:T(8,128)(2,1)} %bitcast.10.token_ref.refs_2_, bf16[4,4,2,64,128]{4,3,2,1,0:T(8,128)(2,1)S(1)} %collective-permute-done.refs_3_, ...), custom_call_target="tpu_custom_call" | custom-call | flops 20000000000 | bytes 6291456 | tf_op jit(solution)/shard_map/pallas_call | solution.py:189
  152.7 16.0 %all_to_all.15 = bf16[8,64,1024]{2,1,0:T(8,128)(2,1)S(1)} all-to-all(bf16[8,64,1024]{2,1,0:T(8,128)(2,1)S(1)} %shard_map.40), channel_id=1, replica_groups={{0,24,32,56,64,88,96,120},{8,16,40,48,72,80,104,112},{1,25,33,57,65,89,..., dimensions={0} | all-to-all | bytes 2097152 | tf_op jit(solution)/shard_map/all_to_all | solution.py:217
  168.7 1.1 copy.6
  (6 shorter events, 0.1 us)
Async XLA Ops:
  2.0 19.7 %all-to-all-start = ((bf16[16,2,64,128]{3,2,1,0:T(8,128)(2,1)}), bf16[16,2,64,128]{3,2,1,0:T(8,128)(2,1)}, u32[]{:S(2)}, u32[]{:S(2)}) async-start(bf16[16,2,64,128]{3,2,1,0:T(8,128)(2,1)} %shard_map.38), calls=%async_computation | async-start | bytes 1048576 | tf_op jit(solution)/shard_map/all_to_all | solution.py:223
  22.8 10.8 %collective-permute-start.5 = (bf16[2,4,2,64,128]{4,3,2,1,0:T(8,128)(2,1)S(1)}, bf16[2,4,2,64,128]{4,3,2,1,0:T(8,128)(2,1)S(1)}, u32[]{:S(2)}, u32[]{:S(2)}) collective-permute-start(bf16[2,4,2,64,128]{4,3,2,1,0:T(8,128)(2,1)S(1)} %bitcast.19), channel_id=1, source_target_pairs={{4,0},{5,1},{6,2},{7,3},{0,4},{1,5},{2,6},{3,7},{12,8},{13,9},{14,... | collective-permute-start | bytes 786440 | tf_op jit(solution)/shard_map/ppermute | solution.py:205
  25.9 16.3 %collective-permute-start.3 = (bf16[4,4,2,64,128]{4,3,2,1,0:T(8,128)(2,1)}, bf16[4,4,2,64,128]{4,3,2,1,0:T(8,128)(2,1)S(1)}, u32[]{:S(2)}, u32[]{:S(2)}) collective-permute-start(bf16[4,4,2,64,128]{4,3,2,1,0:T(8,128)(2,1)} %bitcast.10.token_ref.refs_2_), channel_id=1, source_target_pairs={{6,0},{7,1},{0,2},{1,3},{2,4},{3,5},{4,6},{5,7},{14,8},{15,9},{8,1... | collective-permute-start | bytes 1572872 | tf_op jit(solution)/shard_map/ppermute | solution.py:205
  26.5 15.8 %collective-permute-start.1 = (bf16[4,4,2,64,128]{4,3,2,1,0:T(8,128)(2,1)}, bf16[4,4,2,64,128]{4,3,2,1,0:T(8,128)(2,1)S(1)}, u32[]{:S(2)}, u32[]{:S(2)}) collective-permute-start(bf16[4,4,2,64,128]{4,3,2,1,0:T(8,128)(2,1)} %bitcast.10.token_ref.refs_2_), channel_id=1, source_target_pairs={{2,0},{3,1},{4,2},{5,3},{6,4},{7,5},{0,6},{1,7},{10,8},{11,9},{12,... | collective-permute-start | bytes 1572872 | tf_op jit(solution)/shard_map/ppermute | solution.py:205
  33.6 6.4 %collective-permute-start.6 = (bf16[2,4,2,64,128]{4,3,2,1,0:T(8,128)(2,1)S(1)}, bf16[2,4,2,64,128]{4,3,2,1,0:T(8,128)(2,1)S(1)}, u32[]{:S(2)}, u32[]{:S(2)}) collective-permute-start(bf16[2,4,2,64,128]{4,3,2,1,0:T(8,128)(2,1)S(1)} %collective-permute-done.5), channel_id=1, source_target_pairs={{8,0},{0,8},{24,16},{16,24},{40,32},{32,40},{56,48},{48,56},{72,64... | collective-permute-start | bytes 786440 | tf_op jit(solution)/shard_map/ppermute | solution.py:209
  34.2 15.3 %all-to-all-start.1 = ((bf16[8,512,128]{2,1,0:T(8,128)(2,1)}), bf16[8,512,128]{2,1,0:T(8,128)(2,1)S(1)}, u32[]{:S(2)}, u32[]{:S(2)}) async-start(bf16[8,512,128]{2,1,0:T(8,128)(2,1)} %shard_map.39), calls=%async_computation.1 | async-start | bytes 2097152 | tf_op jit(solution)/shard_map/all_to_all | solution.py:217
  37.8 5.0 %collective-permute-start = (bf16[4,4,2,64,128]{4,3,2,1,0:T(8,128)(2,1)}, bf16[4,4,2,64,128]{4,3,2,1,0:T(8,128)(2,1)S(1)}, u32[]{:S(2)}, u32[]{:S(2)}) collective-permute-start(bf16[4,4,2,64,128]{4,3,2,1,0:T(8,128)(2,1)} %bitcast.10.token_ref.refs_2_), channel_id=1, source_target_pairs={{1,0},{0,1},{3,2},{2,3},{5,4},{4,5},{7,6},{6,7},{9,8},{8,9},{11,10... | collective-permute-start | bytes 1572872 | tf_op jit(solution)/shard_map/ppermute | solution.py:213
  40.1 9.4 %collective-permute-start.7 = (bf16[4,4,2,64,128]{4,3,2,1,0:T(8,128)(2,1)S(1)}, bf16[4,4,2,64,128]{4,3,2,1,0:T(8,128)(2,1)}, u32[]{:S(2)}, u32[]{:S(2)}) collective-permute-start(bf16[4,4,2,64,128]{4,3,2,1,0:T(8,128)(2,1)S(1)} %pad_maximum_fusion.refs_8_), channel_id=1, source_target_pairs={{1,0},{0,1},{3,2},{2,3},{5,4},{4,5},{7,6},{6,7},{9,8},{8,9},{11,10... | collective-permute-start | bytes 1572872 | tf_op jit(solution)/shard_map/ppermute | solution.py:213
  42.2 7.3 %collective-permute-start.4 = (bf16[4,4,2,64,128]{4,3,2,1,0:T(8,128)(2,1)S(1)}, bf16[4,4,2,64,128]{4,3,2,1,0:T(8,128)(2,1)}, u32[]{:S(2)}, u32[]{:S(2)}) collective-permute-start(bf16[4,4,2,64,128]{4,3,2,1,0:T(8,128)(2,1)S(1)} %collective-permute-done.3.refs_6_), channel_id=1, source_target_pairs={{1,0},{0,1},{3,2},{2,3},{5,4},{4,5},{7,6},{6,7},{9,8},{8,9},{11,10... | collective-permute-start | bytes 1572872 | tf_op jit(solution)/shard_map/ppermute | solution.py:213
  42.3 7.2 %collective-permute-start.2 = (bf16[4,4,2,64,128]{4,3,2,1,0:T(8,128)(2,1)S(1)}, bf16[4,4,2,64,128]{4,3,2,1,0:T(8,128)(2,1)}, u32[]{:S(2)}, u32[]{:S(2)}) collective-permute-start(bf16[4,4,2,64,128]{4,3,2,1,0:T(8,128)(2,1)S(1)} %collective-permute-done.1.refs_4_), channel_id=1, source_target_pairs={{1,0},{0,1},{3,2},{2,3},{5,4},{4,5},{7,6},{6,7},{9,8},{8,9},{11,10... | collective-permute-start | bytes 1572872 | tf_op jit(solution)/shard_map/ppermute | solution.py:213

commit v3 on v2

--- a/solution.py
+++ b/solution.py
@@ -58,25 +58,10 @@
     )(queries)
 
 
-def after_kernel(array_ref, token_ref, o_ref):
-    del array_ref, token_ref, o_ref
-
-
-def after(array, token):
-    return pl.pallas_call(
-        after_kernel,
-        out_shape=jax.ShapeDtypeStruct(array.shape, array.dtype),
-        in_specs=[pl.BlockSpec(memory_space=pl.ANY)] * 2,
-        out_specs=pl.BlockSpec(memory_space=pl.ANY),
-        input_output_aliases={0: 0},
-        cost_estimate=pl.CostEstimate(flops=5 * 10**9, bytes_accessed=0, transcendentals=0),
-    )(array, token)
-
-
 def attend_kernel(*refs):
     where_ref, q_ref = refs[:2]
     block_refs = refs[2:10]
-    o_ref, acc, bias, top = refs[10:]
+    o_ref, acc_pairs, bias, top, extremes = refs[10:]
     inner = where_ref[0]
     token = lax.broadcasted_iota(jnp.int32, (TOK, TOK), 0)
     key = lax.broadcasted_iota(jnp.int32, (TOK, TOK), 1)
@@ -85,7 +70,11 @@
         bias[:, b * TOK : (b + 1) * TOK] = jnp.where(ahead * TOK + key <= token, 0.0, HIDDEN)
 
     def load(part, quads):
-        return jnp.concatenate([r[(*quad, part)] for quad in quads for r in block_refs], axis=0)
+        def rows(y, z):
+            turned = lax.rem(y + 2 * inner, 4)
+            return [r[y if b < 6 else turned, z, part] for b, r in enumerate(block_refs)]
+
+        return jnp.concatenate([piece for quad in quads for piece in rows(*quad)], axis=0)
 
     def scores(y, row, rows, quads, masked):
         x = (
@@ -112,6 +101,7 @@
         )
 
     def run(y, jobs, fresh):
+        acc = acc_pairs.at[y % 2]
         x = scores(y, jobs[0][0], STEP, *jobs[0][1:])
         for n, (row, quads, _) in enumerate(jobs):
             weights = jnp.exp2(x)
@@ -125,15 +115,24 @@
         jobs = [
             (row, [(y, z) for z in range(zs[row // CHUNK] + 1)], True) for row in range(0, PAIR, STEP)
         ]
+        finish(jnp.maximum(y, 1) - 1)
         run(y, jobs, True)
 
-    def store(y, m):
+    def store(y, m, acc):
         rows = slice(m * CHUNK, (m + 1) * CHUNK)
         out = (acc[rows, :HEAD_DIM] / acc[rows, HEAD_DIM:]).astype(jnp.bfloat16)
         for h in range(GROUP):
             o_ref[2 * y + m, :, h * HEAD_DIM : (h + 1) * HEAD_DIM] = out[h * TOK : (h + 1) * TOK]
 
-    def pair(y, bad):
+    def finish(y):
+        acc = acc_pairs.at[y % 2]
+        for m in range(2):
+            store(y, m, acc)
+        total = acc[:, HEAD_DIM:].reshape(PAIR // 8, 8, HEAD_DIM)
+        extremes[0] = jnp.minimum(extremes[0], jnp.min(total, axis=0))
+        extremes[1] = jnp.maximum(extremes[1], jnp.max(total, axis=0))
+
+    def pair(y, carry):
         pl.when(inner == 0)(lambda: same_y(y, (0, 3)))
         pl.when(inner == 1)(lambda: same_y(y, (1, 2)))
 
@@ -143,16 +142,19 @@
             return carry
 
         lax.fori_loop(0, y, earlier, 0)
-        total = acc[:, HEAD_DIM:]
-        for m in range(2):
-            store(y, m)
-        fine = (total >= LOW) & (total <= HIGH)
-        return jnp.maximum(bad, jnp.max(jnp.where(fine, 0.0, 1.0)))
-
-    bad = lax.fori_loop(0, 4, pair, jnp.float32(0.0))
+        return carry
+
+    acc_pairs[0] = jnp.ones((PAIR, 2 * HEAD_DIM), jnp.float32)
+    extremes[...] = jnp.ones((2, 8, HEAD_DIM), jnp.float32)
+    lax.fori_loop(0, 4, pair, 0)
+    finish(3)
+    fine = (extremes[0] >= LOW) & (extremes[1] <= HIGH)
+    bad = jnp.max(jnp.where(fine, 0.0, 1.0))
 
     @pl.when(bad > 0.0)
     def _():
+        acc = acc_pairs.at[0]
+
         def exact(y, m, quad, first):
             row = pl.multiple_of(m * CHUNK, CHUNK)
             rows = pl.ds(row, CHUNK)
@@ -175,7 +177,7 @@
                 return carry
 
             lax.fori_loop(0, 4 * n + z, others, 0)
-            store(n, m)
+            store(n, m, acc)
 
         def exact_pair(y, carry):
             for m in range(2):
@@ -192,9 +194,10 @@
         in_specs=[pl.BlockSpec(memory_space=pltpu.SMEM)] + [VMEM] * 9,
         out_specs=VMEM,
         scratch_shapes=[
-            pltpu.VMEM((PAIR, 2 * HEAD_DIM), jnp.float32),
+            pltpu.VMEM((2, PAIR, 2 * HEAD_DIM), jnp.float32),
             pltpu.VMEM((TOK, 8 * TOK), jnp.float32),
             pltpu.VMEM((CHUNK, HEAD_DIM), jnp.float32),
+            pltpu.VMEM((2, 8, HEAD_DIM), jnp.float32),
         ],
         compiler_params=pltpu.CompilerParams(vmem_limit_bytes=20 * 2**20),
         cost_estimate=pl.CostEstimate(flops=2 * 10**10, bytes_accessed=6 * 2**20, transcendentals=2 * 10**7),
@@ -225,14 +228,15 @@
     q, own = lax.optimization_barrier((q, own))
     own = own.reshape(4, 4, 2, TOK, HEAD_DIM)
     other = swap(own)
-    q = trade(after(q, own)).reshape(4, PAIR, HEAD_DIM)
+    q = trade(q).reshape(4, PAIR, HEAD_DIM)
     inner = (z == 1) | (z == 2)
     half = around(jnp.where(inner, own[2:], own[:2]), 2)
     rest = across(half)
-    far = jnp.concatenate([jnp.where(inner, rest, half), jnp.where(inner, half, rest)], axis=0)
+    far = jnp.concatenate([half, rest])
+    far_other = swap(far)
     blocks, slots = [own, other], [xc, xc ^ 1]
     for step, block in ((1, around(own, 1)), (3, around(own, 3)), (2, far)):
-        blocks += [block, swap(block)]
+        blocks += [block, far_other if step == 2 else swap(block)]
         slots += [(xc + 2 * step) % 8, (xc + 2 * step) % 8 ^ 1]
     where = jnp.stack([jnp.where(inner, 1, 0), xc] + slots).astype(jnp.int32)
     out = trade(attend(where, q, blocks))

time: 170 us -> 166 us (0.976)
  waiting for transfers between devices: 24.5 us -> 21.6 us
    ppermute x1, waiting for transfers between devices: 2.15 us -> 5.78 us  [across(): return lax.ppermute(array, 'yz', [(n ^ 1, n) for n in range(16)])]
    ppermute x3, waiting for transfers between devices: 6.57 us -> 3.06 us  [around(): lax.ppermute(array, 'xc', [((n + 2 * step) % 8, n) for n in range(8)])]
    all_to_all x1, waiting for transfers between devices: 6.65 us -> 3.7 us  [trade(): lax.all_to_all(array, 'yz', split_axis=0, concat_axis=0, tiled=True, axis...]
where the time goes in v3:
time: 166 us; the launch traced here: 165 us
  Pallas kernels  107 us (64%)
  waiting for transfers between devices  21.6 us (13%)
  starting transfers between devices  19.1 us (12%)
  blocking collectives  16 us (10%)
    pallas_call x1, Pallas kernels, attend(): pl.pallas_call(attend_kernel, out_shape=jax.ShapeDtypeStruct((8, TOK, GRO...  103 us
    all_to_all x1, blocking collectives, trade(): lax.all_to_all(array, 'yz', split_axis=0, concat_axis=0, tiled=True, axis...  16 us
    all_to_all x1, waiting for transfers between devices, on_device(): own = lax.all_to_all(kv, 'yz', split_axis=0, concat_axis=0, tiled=True)  9.09 us
    all_to_all x1, starting transfers between devices, on_device(): own = lax.all_to_all(kv, 'yz', split_axis=0, concat_axis=0, tiled=True)  8.13 us
    ppermute x3, starting transfers between devices, around(): lax.ppermute(array, 'xc', [((n + 2 * step) % 8, n) for n in range(8)])  6.34 us
    ppermute x1, waiting for transfers between devices, across(): return lax.ppermute(array, 'yz', [(n ^ 1, n) for n in range(16)])  5.78 us
    all_to_all x1, waiting for transfers between devices, trade(): lax.all_to_all(array, 'yz', split_axis=0, concat_axis=0, tiled=True, axis...  3.7 us
    all_to_all x1, starting transfers between devices, trade(): lax.all_to_all(array, 'yz', split_axis=0, concat_axis=0, tiled=True, axis...  3.56 us
  transfers between devices with their start and end apart: 10, of which 6 were waited for; matrix products, arithmetic and copies ran while one was open for 0% of the time, Pallas kernels for 1%

profile of v3, /device:TPU:0, one launch (start us, length us, event | category | flops | bytes accessed | tf_op | source)
XLA Modules:
  0.0 165.2 jit_solution(7475445624637864795)
XLA Ops:
  0.0 2.0 %shard_map.38 = bf16[16,2,64,128]{3,2,1,0:T(8,128)(2,1)} custom-call(bf16[64,1024]{1,0:T(8,128)(2,1)} %k_ref.1, bf16[64,1024]{1,0:T(8,128)(2,1)} %v_ref.1), custom_call_target="tpu_custom_call" | custom-call | tf_op jit(solution)/shard_map/pallas_call | solution.py:42
  2.0 8.1 %all-to-all-start = ((bf16[16,2,64,128]{3,2,1,0:T(8,128)(2,1)}), bf16[16,2,64,128]{3,2,1,0:T(8,128)(2,1)S(1)}, u32[]{:S(2)}, u32[]{:S(2)}) async-start(bf16[16,2,64,128]{3,2,1,0:T(8,128)(2,1)} %shard_map.38), calls=%async_computation | async-start | bytes 1048576 | tf_op jit(solution)/shard_map/all_to_all | solution.py:226
  10.1 2.4 %shard_map.37 = bf16[64,64,128]{2,1,0:T(8,128)(2,1)} custom-call(bf16[64,8192]{1,0:T(8,128)(2,1)} %q_ref.1), custom_call_target="tpu_custom_call" | custom-call | tf_op jit(solution)/shard_map/pallas_call | solution.py:55
  12.5 9.1 %all-to-all-done = bf16[16,2,64,128]{3,2,1,0:T(8,128)(2,1)S(1)} async-done(((bf16[16,2,64,128]{3,2,1,0:T(8,128)(2,1)}), bf16[16,2,64,128]{3,2,1,0:T(8,128)(2,1)S(1)}, u32[]{:S(2)}, u32[]{:S(2)}) %all-to-all-start) | async-done | bytes 524320 | tf_op jit(solution)/shard_map/all_to_all | solution.py:226
  21.6 3.1 %collective-permute-start.5 = (bf16[2,4,2,64,128]{4,3,2,1,0:T(8,128)(2,1)S(1)}, bf16[2,4,2,64,128]{4,3,2,1,0:T(8,128)(2,1)S(1)}, u32[]{:S(2)}, u32[]{:S(2)}) collective-permute-start(bf16[2,4,2,64,128]{4,3,2,1,0:T(8,128)(2,1)S(1)} %bitcast.23), channel_id=1, source_target_pairs={{4,0},{5,1},{6,2},{7,3},{0,4},{1,5},{2,6},{3,7},{12,8},{13,9},{14,... | collective-permute-start | bytes 786440 | tf_op jit(solution)/shard_map/ppermute | solution.py:208
  24.8 0.6 collective-permute-start.3
  25.3 2.6 %collective-permute-start.1 = (bf16[4,4,2,64,128]{4,3,2,1,0:T(8,128)(2,1)S(1)}, bf16[4,4,2,64,128]{4,3,2,1,0:T(8,128)(2,1)S(1)}, u32[]{:S(2)}, u32[]{:S(2)}) collective-permute-start(bf16[4,4,2,64,128]{4,3,2,1,0:T(8,128)(2,1)S(1)} %bitcast.17), channel_id=1, source_target_pairs={{2,0},{3,1},{4,2},{5,3},{6,4},{7,5},{0,6},{1,7},{10,8},{11,9},{12,... | collective-permute-start | bytes 1572872 | tf_op jit(solution)/shard_map/ppermute | solution.py:208
  28.0 3.6 %all-to-all-start.1 = ((bf16[8,512,128]{2,1,0:T(8,128)(2,1)}), bf16[8,512,128]{2,1,0:T(8,128)(2,1)S(1)}, u32[]{:S(2)}, u32[]{:S(2)}) async-start(bf16[8,512,128]{2,1,0:T(8,128)(2,1)} %bitcast.21), calls=%async_computation.1 | async-start | bytes 2097152 | tf_op jit(solution)/shard_map/all_to_all | solution.py:220
  31.6 0.9 collective-permute-done.5
  32.5 0.6 collective-permute-start.6
  33.0 0.0 collective-permute-start
  33.1 5.8 %collective-permute-done.6 = bf16[2,4,2,64,128]{4,3,2,1,0:T(8,128)(2,1)S(1)} collective-permute-done((bf16[2,4,2,64,128]{4,3,2,1,0:T(8,128)(2,1)S(1)}, bf16[2,4,2,64,128]{4,3,2,1,0:T(8,128)(2,1)S(1)}, u32[]{:S(2)}, u32[]{:S(2)}) %collective-permute-start.6) | collective-permute-done | bytes 262176 | tf_op jit(solution)/shard_map/ppermute | solution.py:212
  38.9 0.1 collective-permute-start.7
  39.0 2.1 %collective-permute-done.3.refs_6_ = bf16[4,4,2,64,128]{4,3,2,1,0:T(8,128)(2,1)S(1)} collective-permute-done((bf16[4,4,2,64,128]{4,3,2,1,0:T(8,128)(2,1)S(1)}, bf16[4,4,2,64,128]{4,3,2,1,0:T(8,128)(2,1)S(1)}, u32[]{:S(2)}, u32[]{:S(2)}) %collective-permute-start.3) | collective-permute-done | bytes 524320 | tf_op jit(solution)/shard_map/ppermute | solution.py:208
  41.0 0.0 collective-permute-start.4
  41.1 0.1 collective-permute-done.1.refs_4_
  41.1 0.4 collective-permute-start.2
  41.6 0.1 stack.40.refs_0_
  41.6 0.0 collective-permute-done.refs_3_
  41.7 3.7 %all-to-all-done.1 = bf16[8,512,128]{2,1,0:T(8,128)(2,1)S(1)} async-done(((bf16[8,512,128]{2,1,0:T(8,128)(2,1)}), bf16[8,512,128]{2,1,0:T(8,128)(2,1)S(1)}, u32[]{:S(2)}, u32[]{:S(2)}) %all-to-all-start.1) | async-done | bytes 1048608 | tf_op jit(solution)/shard_map/all_to_all | solution.py:220
  45.4 0.0 collective-permute-done.7.refs_9_
  45.4 102.8 %shard_map.39 = bf16[8,64,1024]{2,1,0:T(8,128)(2,1)S(1)} custom-call(s32[10]{0:T(128)S(1)} %stack.40.refs_0_, bf16[4,1024,128]{2,1,0:T(8,128)(2,1)S(1)} %bitcast.20, bf16[4,4,2,64,128]{4,3,2,1,0:T(8,128)(2,1)S(1)} %bitcast.19, bf16[4,4,2,64,128]{4,3,2,1,0:T(8,128)(2,1)} %collective-permute-done.refs_3_, ...), custom_call_target="tpu_custom_call" | custom-call | flops 20000000000 | bytes 6291456 | tf_op jit(solution)/shard_map/pallas_call | solution.py:191
  148.2 16.0 %all_to_all.15 = bf16[8,64,1024]{2,1,0:T(8,128)(2,1)S(1)} all-to-all(bf16[8,64,1024]{2,1,0:T(8,128)(2,1)S(1)} %shard_map.39), channel_id=1, replica_groups={{0,24,32,56,64,88,96,120},{8,16,40,48,72,80,104,112},{1,25,33,57,65,89,..., dimensions={0} | all-to-all | bytes 2097152 | tf_op jit(solution)/shard_map/all_to_all | solution.py:220
  164.1 1.1 copy.5
  (5 shorter events, 0.1 us)
Async XLA Ops:
  2.0 19.6 %all-to-all-start = ((bf16[16,2,64,128]{3,2,1,0:T(8,128)(2,1)}), bf16[16,2,64,128]{3,2,1,0:T(8,128)(2,1)S(1)}, u32[]{:S(2)}, u32[]{:S(2)}) async-start(bf16[16,2,64,128]{3,2,1,0:T(8,128)(2,1)} %shard_map.38), calls=%async_computation | async-start | bytes 1048576 | tf_op jit(solution)/shard_map/all_to_all | solution.py:226
  21.6 10.8 %collective-permute-start.5 = (bf16[2,4,2,64,128]{4,3,2,1,0:T(8,128)(2,1)S(1)}, bf16[2,4,2,64,128]{4,3,2,1,0:T(8,128)(2,1)S(1)}, u32[]{:S(2)}, u32[]{:S(2)}) collective-permute-start(bf16[2,4,2,64,128]{4,3,2,1,0:T(8,128)(2,1)S(1)} %bitcast.23), channel_id=1, source_target_pairs={{4,0},{5,1},{6,2},{7,3},{0,4},{1,5},{2,6},{3,7},{12,8},{13,9},{14,... | collective-permute-start | bytes 786440 | tf_op jit(solution)/shard_map/ppermute | solution.py:208
  24.8 16.3 %collective-permute-start.3 = (bf16[4,4,2,64,128]{4,3,2,1,0:T(8,128)(2,1)S(1)}, bf16[4,4,2,64,128]{4,3,2,1,0:T(8,128)(2,1)S(1)}, u32[]{:S(2)}, u32[]{:S(2)}) collective-permute-start(bf16[4,4,2,64,128]{4,3,2,1,0:T(8,128)(2,1)S(1)} %bitcast.16), channel_id=1, source_target_pairs={{6,0},{7,1},{0,2},{1,3},{2,4},{3,5},{4,6},{5,7},{14,8},{15,9},{8,1... | collective-permute-start | bytes 1572872 | tf_op jit(solution)/shard_map/ppermute | solution.py:208
  25.3 15.8 %collective-permute-start.1 = (bf16[4,4,2,64,128]{4,3,2,1,0:T(8,128)(2,1)S(1)}, bf16[4,4,2,64,128]{4,3,2,1,0:T(8,128)(2,1)S(1)}, u32[]{:S(2)}, u32[]{:S(2)}) collective-permute-start(bf16[4,4,2,64,128]{4,3,2,1,0:T(8,128)(2,1)S(1)} %bitcast.17), channel_id=1, source_target_pairs={{2,0},{3,1},{4,2},{5,3},{6,4},{7,5},{0,6},{1,7},{10,8},{11,9},{12,... | collective-permute-start | bytes 1572872 | tf_op jit(solution)/shard_map/ppermute | solution.py:208
  28.0 17.4 %all-to-all-start.1 = ((bf16[8,512,128]{2,1,0:T(8,128)(2,1)}), bf16[8,512,128]{2,1,0:T(8,128)(2,1)S(1)}, u32[]{:S(2)}, u32[]{:S(2)}) async-start(bf16[8,512,128]{2,1,0:T(8,128)(2,1)} %bitcast.21), calls=%async_computation.1 | async-start | bytes 2097152 | tf_op jit(solution)/shard_map/all_to_all | solution.py:220
  32.5 6.4 %collective-permute-start.6 = (bf16[2,4,2,64,128]{4,3,2,1,0:T(8,128)(2,1)S(1)}, bf16[2,4,2,64,128]{4,3,2,1,0:T(8,128)(2,1)S(1)}, u32[]{:S(2)}, u32[]{:S(2)}) collective-permute-start(bf16[2,4,2,64,128]{4,3,2,1,0:T(8,128)(2,1)S(1)} %collective-permute-done.5), channel_id=1, source_target_pairs={{8,0},{0,8},{24,16},{16,24},{40,32},{32,40},{56,48},{48,56},{72,64... | collective-permute-start | bytes 786440 | tf_op jit(solution)/shard_map/ppermute | solution.py:212
  33.0 8.6 %collective-permute-start = (bf16[4,4,2,64,128]{4,3,2,1,0:T(8,128)(2,1)S(1)}, bf16[4,4,2,64,128]{4,3,2,1,0:T(8,128)(2,1)}, u32[]{:S(2)}, u32[]{:S(2)}) collective-permute-start(bf16[4,4,2,64,128]{4,3,2,1,0:T(8,128)(2,1)S(1)} %bitcast.18), channel_id=1, source_target_pairs={{1,0},{0,1},{3,2},{2,3},{5,4},{4,5},{7,6},{6,7},{9,8},{8,9},{11,10... | collective-permute-start | bytes 1572872 | tf_op jit(solution)/shard_map/ppermute | solution.py:216
  38.9 6.5 %collective-permute-start.7 = (bf16[4,4,2,64,128]{4,3,2,1,0:T(8,128)(2,1)S(1)}, bf16[4,4,2,64,128]{4,3,2,1,0:T(8,128)(2,1)}, u32[]{:S(2)}, u32[]{:S(2)}) collective-permute-start(bf16[4,4,2,64,128]{4,3,2,1,0:T(8,128)(2,1)S(1)} %constant_dynamic-update-slice_fusion.refs_8_), channel_id=1, source_target_pairs={{1,0},{0,1},{3,2},{2,3},{5,4},{4,5},{7,6},{6,7},{9,8},{8,9},{11,10... | collective-permute-start | bytes 1572872 | tf_op jit(solution)/shard_map/ppermute | solution.py:216
  41.0 4.3 %collective-permute-start.4 = (bf16[4,4,2,64,128]{4,3,2,1,0:T(8,128)(2,1)S(1)}, bf16[4,4,2,64,128]{4,3,2,1,0:T(8,128)(2,1)}, u32[]{:S(2)}, u32[]{:S(2)}) collective-permute-start(bf16[4,4,2,64,128]{4,3,2,1,0:T(8,128)(2,1)S(1)} %collective-permute-done.3.refs_6_), channel_id=1, source_target_pairs={{1,0},{0,1},{3,2},{2,3},{5,4},{4,5},{7,6},{6,7},{9,8},{8,9},{11,10... | collective-permute-start | bytes 1572872 | tf_op jit(solution)/shard_map/ppermute | solution.py:216
  41.1 4.2 %collective-permute-start.2 = (bf16[4,4,2,64,128]{4,3,2,1,0:T(8,128)(2,1)S(1)}, bf16[4,4,2,64,128]{4,3,2,1,0:T(8,128)(2,1)}, u32[]{:S(2)}, u32[]{:S(2)}) collective-permute-start(bf16[4,4,2,64,128]{4,3,2,1,0:T(8,128)(2,1)S(1)} %collective-permute-done.1.refs_4_), channel_id=1, source_target_pairs={{1,0},{0,1},{3,2},{2,3},{5,4},{4,5},{7,6},{6,7},{9,8},{8,9},{11,10... | collective-permute-start | bytes 1572872 | tf_op jit(solution)/shard_map/ppermute | solution.py:216

commit v4 on v3

--- a/solution.py
+++ b/solution.py
@@ -58,6 +58,21 @@
     )(queries)
 
 
+def after_kernel(array_ref, token_ref, o_ref):
+    del array_ref, token_ref, o_ref
+
+
+def after(array, token):
+    return pl.pallas_call(
+        after_kernel,
+        out_shape=jax.ShapeDtypeStruct(array.shape, array.dtype),
+        in_specs=[pl.BlockSpec(memory_space=pl.ANY)] * 2,
+        out_specs=pl.BlockSpec(memory_space=pl.ANY),
+        input_output_aliases={0: 0},
+        cost_estimate=pl.CostEstimate(flops=5 * 10**9, bytes_accessed=0, transcendentals=0),
+    )(array, token)
+
+
 def attend_kernel(*refs):
     where_ref, q_ref = refs[:2]
     block_refs = refs[2:10]
@@ -70,11 +85,7 @@
         bias[:, b * TOK : (b + 1) * TOK] = jnp.where(ahead * TOK + key <= token, 0.0, HIDDEN)
 
     def load(part, quads):
-        def rows(y, z):
-            turned = lax.rem(y + 2 * inner, 4)
-            return [r[y if b < 6 else turned, z, part] for b, r in enumerate(block_refs)]
-
-        return jnp.concatenate([piece for quad in quads for piece in rows(*quad)], axis=0)
+        return jnp.concatenate([r[(*quad, part)] for quad in quads for r in block_refs], axis=0)
 
     def scores(y, row, rows, quads, masked):
         x = (
@@ -228,15 +239,14 @@
     q, own = lax.optimization_barrier((q, own))
     own = own.reshape(4, 4, 2, TOK, HEAD_DIM)
     other = swap(own)
-    q = trade(q).reshape(4, PAIR, HEAD_DIM)
+    q = trade(after(q, own[0, 0, 0, :16])).reshape(4, PAIR, HEAD_DIM)
     inner = (z == 1) | (z == 2)
     half = around(jnp.where(inner, own[2:], own[:2]), 2)
     rest = across(half)
-    far = jnp.concatenate([half, rest])
-    far_other = swap(far)
+    far = jnp.concatenate([jnp.where(inner, rest, half), jnp.where(inner, half, rest)], axis=0)
     blocks, slots = [own, other], [xc, xc ^ 1]
     for step, block in ((1, around(own, 1)), (3, around(own, 3)), (2, far)):
-        blocks += [block, far_other if step == 2 else swap(block)]
+        blocks += [block, swap(block)]
         slots += [(xc + 2 * step) % 8, (xc + 2 * step) % 8 ^ 1]
     where = jnp.stack([jnp.where(inner, 1, 0), xc] + slots).astype(jnp.int32)
     out = trade(attend(where, q, blocks))

time: 166 us -> 169 us (1.018)
  waiting for transfers between devices: 21.6 us -> 23.9 us
    ppermute x1, waiting for transfers between devices: 5.78 us -> 2.15 us  [across(): return lax.ppermute(array, 'yz', [(n ^ 1, n) for n in range(16)])]
    all_to_all x1, waiting for transfers between devices: 3.7 us -> 6.65 us  [trade(): lax.all_to_all(array, 'yz', split_axis=0, concat_axis=0, tiled=True, axis...]
    ppermute x3, waiting for transfers between devices: 3.06 us -> 5.98 us  [around(): lax.ppermute(array, 'xc', [((n + 2 * step) % 8, n) for n in range(8)])]
where the time goes in v4:
time: 169 us; the launch traced here: 168 us
  Pallas kernels  107 us (63%)
  waiting for transfers between devices  23.9 us (14%)
  starting transfers between devices  19.2 us (11%)
  blocking collectives  16.1 us (10%)
  local copies, waits for them, and re-layouts  1.73 us (1%)
    pallas_call x1, Pallas kernels, attend(): pl.pallas_call(attend_kernel, out_shape=jax.ShapeDtypeStruct((8, TOK, GRO...  103 us
    all_to_all x1, blocking collectives, trade(): lax.all_to_all(array, 'yz', split_axis=0, concat_axis=0, tiled=True, axis...  16.1 us
    all_to_all x1, waiting for transfers between devices, on_device(): own = lax.all_to_all(kv, 'yz', split_axis=0, concat_axis=0, tiled=True)  9.09 us
    all_to_all x1, starting transfers between devices, on_device(): own = lax.all_to_all(kv, 'yz', split_axis=0, concat_axis=0, tiled=True)  8.13 us
    all_to_all x1, waiting for transfers between devices, trade(): lax.all_to_all(array, 'yz', split_axis=0, concat_axis=0, tiled=True, axis...  6.65 us
    ppermute x3, starting transfers between devices, around(): lax.ppermute(array, 'xc', [((n + 2 * step) % 8, n) for n in range(8)])  6.34 us
    ppermute x3, waiting for transfers between devices, around(): lax.ppermute(array, 'xc', [((n + 2 * step) % 8, n) for n in range(8)])  5.98 us
    all_to_all x1, starting transfers between devices, trade(): lax.all_to_all(array, 'yz', split_axis=0, concat_axis=0, tiled=True, axis...  3.56 us
  transfers between devices with their start and end apart: 10, of which 6 were waited for; matrix products, arithmetic and copies ran while one was open for 0% of the time, Pallas kernels for 1%

profile of v4, /device:TPU:0, one launch (start us, length us, event | category | flops | bytes accessed | tf_op | source)
XLA Modules:
  0.0 168.2 jit_solution(733170527962618088)
XLA Ops:
  0.0 2.0 %shard_map.38 = bf16[16,2,64,128]{3,2,1,0:T(8,128)(2,1)} custom-call(bf16[64,1024]{1,0:T(8,128)(2,1)} %k_ref.1, bf16[64,1024]{1,0:T(8,128)(2,1)} %v_ref.1), custom_call_target="tpu_custom_call" | custom-call | tf_op jit(solution)/shard_map/pallas_call | solution.py:42
  2.0 8.1 %all-to-all-start = ((bf16[16,2,64,128]{3,2,1,0:T(8,128)(2,1)}), bf16[16,2,64,128]{3,2,1,0:T(8,128)(2,1)S(1)}, u32[]{:S(2)}, u32[]{:S(2)}) async-start(bf16[16,2,64,128]{3,2,1,0:T(8,128)(2,1)} %shard_map.38), calls=%async_computation | async-start | bytes 1048576 | tf_op jit(solution)/shard_map/all_to_all | solution.py:237
  10.2 2.4 %shard_map.37 = bf16[64,64,128]{2,1,0:T(8,128)(2,1)} custom-call(bf16[64,8192]{1,0:T(8,128)(2,1)} %q_ref.1), custom_call_target="tpu_custom_call" | custom-call | tf_op jit(solution)/shard_map/pallas_call | solution.py:55
  12.5 9.1 %all-to-all-done = bf16[16,2,64,128]{3,2,1,0:T(8,128)(2,1)S(1)} async-done(((bf16[16,2,64,128]{3,2,1,0:T(8,128)(2,1)}), bf16[16,2,64,128]{3,2,1,0:T(8,128)(2,1)S(1)}, u32[]{:S(2)}, u32[]{:S(2)}) %all-to-all-start) | async-done | bytes 524320 | tf_op jit(solution)/shard_map/all_to_all | solution.py:237
  21.7 3.1 %collective-permute-start.5 = (bf16[2,4,2,64,128]{4,3,2,1,0:T(8,128)(2,1)S(1)}, bf16[2,4,2,64,128]{4,3,2,1,0:T(8,128)(2,1)S(1)}, u32[]{:S(2)}, u32[]{:S(2)}) collective-permute-start(bf16[2,4,2,64,128]{4,3,2,1,0:T(8,128)(2,1)S(1)} %bitcast.26), channel_id=1, source_target_pairs={{4,0},{5,1},{6,2},{7,3},{0,4},{1,5},{2,6},{3,7},{12,8},{13,9},{14,... | collective-permute-start | bytes 786440 | tf_op jit(solution)/shard_map/ppermute | solution.py:219
  24.8 0.6 collective-permute-start.3
  25.4 2.6 %collective-permute-start.1 = (bf16[4,4,2,64,128]{4,3,2,1,0:T(8,128)(2,1)S(1)}, bf16[4,4,2,64,128]{4,3,2,1,0:T(8,128)(2,1)S(1)}, u32[]{:S(2)}, u32[]{:S(2)}) collective-permute-start(bf16[4,4,2,64,128]{4,3,2,1,0:T(8,128)(2,1)S(1)} %bitcast.19), channel_id=1, source_target_pairs={{2,0},{3,1},{4,2},{5,3},{6,4},{7,5},{0,6},{1,7},{10,8},{11,9},{12,... | collective-permute-start | bytes 1572872 | tf_op jit(solution)/shard_map/ppermute | solution.py:219
  28.0 0.6 slice_bitcast_fusion.token_ref
  28.6 3.9 %collective-permute-done.5 = bf16[2,4,2,64,128]{4,3,2,1,0:T(8,128)(2,1)S(1)} collective-permute-done((bf16[2,4,2,64,128]{4,3,2,1,0:T(8,128)(2,1)S(1)}, bf16[2,4,2,64,128]{4,3,2,1,0:T(8,128)(2,1)S(1)}, u32[]{:S(2)}, u32[]{:S(2)}) %collective-permute-start.5) | collective-permute-done | bytes 262176 | tf_op jit(solution)/shard_map/ppermute | solution.py:219
  32.5 0.6 collective-permute-start.6
  33.1 3.6 %all-to-all-start.1 = ((bf16[8,512,128]{2,1,0:T(8,128)(2,1)}), bf16[8,512,128]{2,1,0:T(8,128)(2,1)S(1)}, u32[]{:S(2)}, u32[]{:S(2)}) async-start(bf16[8,512,128]{2,1,0:T(8,128)(2,1)} %shard_map.39), calls=%async_computation.1 | async-start | bytes 2097152 | tf_op jit(solution)/shard_map/all_to_all | solution.py:231
  36.6 0.1 collective-permute-start
  36.7 2.1 %collective-permute-done.6 = bf16[2,4,2,64,128]{4,3,2,1,0:T(8,128)(2,1)S(1)} collective-permute-done((bf16[2,4,2,64,128]{4,3,2,1,0:T(8,128)(2,1)S(1)}, bf16[2,4,2,64,128]{4,3,2,1,0:T(8,128)(2,1)S(1)}, u32[]{:S(2)}, u32[]{:S(2)}) %collective-permute-start.6) | collective-permute-done | bytes 262176 | tf_op jit(solution)/shard_map/ppermute | solution.py:223
  39.0 0.1 collective-permute-start.7
  39.1 2.0 %collective-permute-done.3.refs_6_ = bf16[4,4,2,64,128]{4,3,2,1,0:T(8,128)(2,1)S(1)} collective-permute-done((bf16[4,4,2,64,128]{4,3,2,1,0:T(8,128)(2,1)S(1)}, bf16[4,4,2,64,128]{4,3,2,1,0:T(8,128)(2,1)S(1)}, u32[]{:S(2)}, u32[]{:S(2)}) %collective-permute-start.3) | collective-permute-done | bytes 524320 | tf_op jit(solution)/shard_map/ppermute | solution.py:219
  41.1 0.0 collective-permute-start.4
  41.1 0.1 collective-permute-done.1.refs_4_
  41.2 0.4 collective-permute-start.2
  41.6 0.1 stack.40.refs_0_
  41.7 0.0 collective-permute-done.refs_3_
  41.7 6.7 %all-to-all-done.1 = bf16[8,512,128]{2,1,0:T(8,128)(2,1)S(1)} async-done(((bf16[8,512,128]{2,1,0:T(8,128)(2,1)}), bf16[8,512,128]{2,1,0:T(8,128)(2,1)S(1)}, u32[]{:S(2)}, u32[]{:S(2)}) %all-to-all-start.1) | async-done | bytes 1048608 | tf_op jit(solution)/shard_map/all_to_all | solution.py:231
  48.3 102.7 %shard_map.40 = bf16[8,64,1024]{2,1,0:T(8,128)(2,1)S(1)} custom-call(s32[10]{0:T(128)S(1)} %stack.40.refs_0_, bf16[4,1024,128]{2,1,0:T(8,128)(2,1)S(1)} %bitcast.23, bf16[4,4,2,64,128]{4,3,2,1,0:T(8,128)(2,1)S(1)} %bitcast.22, bf16[4,4,2,64,128]{4,3,2,1,0:T(8,128)(2,1)} %collective-permute-done.refs_3_, ...), custom_call_target="tpu_custom_call" | custom-call | flops 20000000000 | bytes 6291456 | tf_op jit(solution)/shard_map/pallas_call | solution.py:202
  151.1 16.1 %all_to_all.15 = bf16[8,64,1024]{2,1,0:T(8,128)(2,1)S(1)} all-to-all(bf16[8,64,1024]{2,1,0:T(8,128)(2,1)S(1)} %shard_map.40), channel_id=1, replica_groups={{0,24,32,56,64,88,96,120},{8,16,40,48,72,80,104,112},{1,25,33,57,65,89,..., dimensions={0} | all-to-all | bytes 2097152 | tf_op jit(solution)/shard_map/all_to_all | solution.py:231
  167.1 1.1 copy.6
  (7 shorter events, 0.1 us)
Async XLA Ops:
  2.0 19.6 %all-to-all-start = ((bf16[16,2,64,128]{3,2,1,0:T(8,128)(2,1)}), bf16[16,2,64,128]{3,2,1,0:T(8,128)(2,1)S(1)}, u32[]{:S(2)}, u32[]{:S(2)}) async-start(bf16[16,2,64,128]{3,2,1,0:T(8,128)(2,1)} %shard_map.38), calls=%async_computation | async-start | bytes 1048576 | tf_op jit(solution)/shard_map/all_to_all | solution.py:237
  21.7 10.8 %collective-permute-start.5 = (bf16[2,4,2,64,128]{4,3,2,1,0:T(8,128)(2,1)S(1)}, bf16[2,4,2,64,128]{4,3,2,1,0:T(8,128)(2,1)S(1)}, u32[]{:S(2)}, u32[]{:S(2)}) collective-permute-start(bf16[2,4,2,64,128]{4,3,2,1,0:T(8,128)(2,1)S(1)} %bitcast.26), channel_id=1, source_target_pairs={{4,0},{5,1},{6,2},{7,3},{0,4},{1,5},{2,6},{3,7},{12,8},{13,9},{14,... | collective-permute-start | bytes 786440 | tf_op jit(solution)/shard_map/ppermute | solution.py:219
  24.8 16.3 %collective-permute-start.3 = (bf16[4,4,2,64,128]{4,3,2,1,0:T(8,128)(2,1)S(1)}, bf16[4,4,2,64,128]{4,3,2,1,0:T(8,128)(2,1)S(1)}, u32[]{:S(2)}, u32[]{:S(2)}) collective-permute-start(bf16[4,4,2,64,128]{4,3,2,1,0:T(8,128)(2,1)S(1)} %bitcast.18), channel_id=1, source_target_pairs={{6,0},{7,1},{0,2},{1,3},{2,4},{3,5},{4,6},{5,7},{14,8},{15,9},{8,1... | collective-permute-start | bytes 1572872 | tf_op jit(solution)/shard_map/ppermute | solution.py:219
  25.4 15.8 %collective-permute-start.1 = (bf16[4,4,2,64,128]{4,3,2,1,0:T(8,128)(2,1)S(1)}, bf16[4,4,2,64,128]{4,3,2,1,0:T(8,128)(2,1)S(1)}, u32[]{:S(2)}, u32[]{:S(2)}) collective-permute-start(bf16[4,4,2,64,128]{4,3,2,1,0:T(8,128)(2,1)S(1)} %bitcast.19), channel_id=1, source_target_pairs={{2,0},{3,1},{4,2},{5,3},{6,4},{7,5},{0,6},{1,7},{10,8},{11,9},{12,... | collective-permute-start | bytes 1572872 | tf_op jit(solution)/shard_map/ppermute | solution.py:219
  32.5 6.4 %collective-permute-start.6 = (bf16[2,4,2,64,128]{4,3,2,1,0:T(8,128)(2,1)S(1)}, bf16[2,4,2,64,128]{4,3,2,1,0:T(8,128)(2,1)S(1)}, u32[]{:S(2)}, u32[]{:S(2)}) collective-permute-start(bf16[2,4,2,64,128]{4,3,2,1,0:T(8,128)(2,1)S(1)} %collective-permute-done.5), channel_id=1, source_target_pairs={{8,0},{0,8},{24,16},{16,24},{40,32},{32,40},{56,48},{48,56},{72,64... | collective-permute-start | bytes 786440 | tf_op jit(solution)/shard_map/ppermute | solution.py:223
  33.1 15.3 %all-to-all-start.1 = ((bf16[8,512,128]{2,1,0:T(8,128)(2,1)}), bf16[8,512,128]{2,1,0:T(8,128)(2,1)S(1)}, u32[]{:S(2)}, u32[]{:S(2)}) async-start(bf16[8,512,128]{2,1,0:T(8,128)(2,1)} %shard_map.39), calls=%async_computation.1 | async-start | bytes 2097152 | tf_op jit(solution)/shard_map/all_to_all | solution.py:231
  36.6 5.0 %collective-permute-start = (bf16[4,4,2,64,128]{4,3,2,1,0:T(8,128)(2,1)S(1)}, bf16[4,4,2,64,128]{4,3,2,1,0:T(8,128)(2,1)}, u32[]{:S(2)}, u32[]{:S(2)}) collective-permute-start(bf16[4,4,2,64,128]{4,3,2,1,0:T(8,128)(2,1)S(1)} %bitcast.21), channel_id=1, source_target_pairs={{1,0},{0,1},{3,2},{2,3},{5,4},{4,5},{7,6},{6,7},{9,8},{8,9},{11,10... | collective-permute-start | bytes 1572872 | tf_op jit(solution)/shard_map/ppermute | solution.py:227
  39.0 9.4 %collective-permute-start.7 = (bf16[4,4,2,64,128]{4,3,2,1,0:T(8,128)(2,1)S(1)}, bf16[4,4,2,64,128]{4,3,2,1,0:T(8,128)(2,1)}, u32[]{:S(2)}, u32[]{:S(2)}) collective-permute-start(bf16[4,4,2,64,128]{4,3,2,1,0:T(8,128)(2,1)S(1)} %pad_maximum_fusion.refs_8_), channel_id=1, source_target_pairs={{1,0},{0,1},{3,2},{2,3},{5,4},{4,5},{7,6},{6,7},{9,8},{8,9},{11,10... | collective-permute-start | bytes 1572872 | tf_op jit(solution)/shard_map/ppermute | solution.py:227
  41.1 7.3 %collective-permute-start.4 = (bf16[4,4,2,64,128]{4,3,2,1,0:T(8,128)(2,1)S(1)}, bf16[4,4,2,64,128]{4,3,2,1,0:T(8,128)(2,1)}, u32[]{:S(2)}, u32[]{:S(2)}) collective-permute-start(bf16[4,4,2,64,128]{4,3,2,1,0:T(8,128)(2,1)S(1)} %collective-permute-done.3.refs_6_), channel_id=1, source_target_pairs={{1,0},{0,1},{3,2},{2,3},{5,4},{4,5},{7,6},{6,7},{9,8},{8,9},{11,10... | collective-permute-start | bytes 1572872 | tf_op jit(solution)/shard_map/ppermute | solution.py:227
  41.2 7.2 %collective-permute-start.2 = (bf16[4,4,2,64,128]{4,3,2,1,0:T(8,128)(2,1)S(1)}, bf16[4,4,2,64,128]{4,3,2,1,0:T(8,128)(2,1)}, u32[]{:S(2)}, u32[]{:S(2)}) collective-permute-start(bf16[4,4,2,64,128]{4,3,2,1,0:T(8,128)(2,1)S(1)} %collective-permute-done.1.refs_4_), channel_id=1, source_target_pairs={{1,0},{0,1},{3,2},{2,3},{5,4},{4,5},{7,6},{6,7},{9,8},{8,9},{11,10... | collective-permute-start | bytes 1572872 | tf_op jit(solution)/shard_map/ppermute | solution.py:227

commit v5 on v3

--- a/solution.py
+++ b/solution.py
@@ -232,11 +232,11 @@
     inner = (z == 1) | (z == 2)
     half = around(jnp.where(inner, own[2:], own[:2]), 2)
     rest = across(half)
-    far = jnp.concatenate([half, rest])
-    far_other = swap(far)
+    near = [around(own, step) for step in (1, 3)]
+    near[0], near[1], rest = lax.optimization_barrier((near[0], near[1], rest))
     blocks, slots = [own, other], [xc, xc ^ 1]
-    for step, block in ((1, around(own, 1)), (3, around(own, 3)), (2, far)):
-        blocks += [block, far_other if step == 2 else swap(block)]
+    for step, block in ((1, near[0]), (3, near[1]), (2, jnp.concatenate([half, rest]))):
+        blocks += [block, swap(block)]
         slots += [(xc + 2 * step) % 8, (xc + 2 * step) % 8 ^ 1]
     where = jnp.stack([jnp.where(inner, 1, 0), xc] + slots).astype(jnp.int32)
     out = trade(attend(where, q, blocks))

time: 166 us -> 166 us (level)
  no operation moved by 1% of the time
where the time goes in v5:
time: 166 us; the launch traced here: 165 us
  Pallas kernels  107 us (64%)
  waiting for transfers between devices  21.5 us (13%)
  starting transfers between devices  19.3 us (12%)
  blocking collectives  16 us (10%)
    pallas_call x1, Pallas kernels, attend(): pl.pallas_call(attend_kernel, out_shape=jax.ShapeDtypeStruct((8, TOK, GRO...  103 us
    all_to_all x1, blocking collectives, trade(): lax.all_to_all(array, 'yz', split_axis=0, concat_axis=0, tiled=True, axis...  16 us
    all_to_all x1, waiting for transfers between devices, on_device(): own = lax.all_to_all(kv, 'yz', split_axis=0, concat_axis=0, tiled=True)  9.09 us
    all_to_all x1, starting transfers between devices, on_device(): own = lax.all_to_all(kv, 'yz', split_axis=0, concat_axis=0, tiled=True)  8.13 us
    ppermute x3, starting transfers between devices, around(): lax.ppermute(array, 'xc', [((n + 2 * step) % 8, n) for n in range(8)])  6.34 us
    ppermute x1, waiting for transfers between devices, across(): return lax.ppermute(array, 'yz', [(n ^ 1, n) for n in range(16)])  5.78 us
    all_to_all x1, starting transfers between devices, trade(): lax.all_to_all(array, 'yz', split_axis=0, concat_axis=0, tiled=True, axis...  3.56 us
    all_to_all x1, waiting for transfers between devices, trade(): lax.all_to_all(array, 'yz', split_axis=0, concat_axis=0, tiled=True, axis...  3.41 us
  transfers between devices with their start and end apart: 10, of which 6 were waited for; matrix products, arithmetic and copies ran while one was open for 0% of the time, Pallas kernels for 1%

profile of v5, /device:TPU:0, one launch (start us, length us, event | category | flops | bytes accessed | tf_op | source)
XLA Modules:
  0.0 165.2 jit_solution(11971717442473390407)
XLA Ops:
  0.0 2.0 %shard_map.38 = bf16[16,2,64,128]{3,2,1,0:T(8,128)(2,1)} custom-call(bf16[64,1024]{1,0:T(8,128)(2,1)} %k_ref.1, bf16[64,1024]{1,0:T(8,128)(2,1)} %v_ref.1), custom_call_target="tpu_custom_call" | custom-call | tf_op jit(solution)/shard_map/pallas_call | solution.py:42
  2.0 8.1 %all-to-all-start = ((bf16[16,2,64,128]{3,2,1,0:T(8,128)(2,1)}), bf16[16,2,64,128]{3,2,1,0:T(8,128)(2,1)S(1)}, u32[]{:S(2)}, u32[]{:S(2)}) async-start(bf16[16,2,64,128]{3,2,1,0:T(8,128)(2,1)} %shard_map.38), calls=%async_computation | async-start | bytes 1048576 | tf_op jit(solution)/shard_map/all_to_all | solution.py:226
  10.1 2.4 %shard_map.37 = bf16[64,64,128]{2,1,0:T(8,128)(2,1)} custom-call(bf16[64,8192]{1,0:T(8,128)(2,1)} %q_ref.1), custom_call_target="tpu_custom_call" | custom-call | tf_op jit(solution)/shard_map/pallas_call | solution.py:55
  12.5 9.1 %all-to-all-done = bf16[16,2,64,128]{3,2,1,0:T(8,128)(2,1)S(1)} async-done(((bf16[16,2,64,128]{3,2,1,0:T(8,128)(2,1)}), bf16[16,2,64,128]{3,2,1,0:T(8,128)(2,1)S(1)}, u32[]{:S(2)}, u32[]{:S(2)}) %all-to-all-start) | async-done | bytes 524320 | tf_op jit(solution)/shard_map/all_to_all | solution.py:226
  21.6 3.1 %collective-permute-start.3 = (bf16[2,4,2,64,128]{4,3,2,1,0:T(8,128)(2,1)S(1)}, bf16[2,4,2,64,128]{4,3,2,1,0:T(8,128)(2,1)S(1)}, u32[]{:S(2)}, u32[]{:S(2)}) collective-permute-start(bf16[2,4,2,64,128]{4,3,2,1,0:T(8,128)(2,1)S(1)} %bitcast.23), channel_id=1, source_target_pairs={{4,0},{5,1},{6,2},{7,3},{0,4},{1,5},{2,6},{3,7},{12,8},{13,9},{14,... | collective-permute-start | bytes 786440 | tf_op jit(solution)/shard_map/ppermute | solution.py:208
  24.8 0.6 collective-permute-start.2
  25.3 2.6 %collective-permute-start.1 = (bf16[4,4,2,64,128]{4,3,2,1,0:T(8,128)(2,1)S(1)}, bf16[4,4,2,64,128]{4,3,2,1,0:T(8,128)(2,1)S(1)}, u32[]{:S(2)}, u32[]{:S(2)}) collective-permute-start(bf16[4,4,2,64,128]{4,3,2,1,0:T(8,128)(2,1)S(1)} %bitcast.17), channel_id=1, source_target_pairs={{2,0},{3,1},{4,2},{5,3},{6,4},{7,5},{0,6},{1,7},{10,8},{11,9},{12,... | collective-permute-start | bytes 1572872 | tf_op jit(solution)/shard_map/ppermute | solution.py:208
  28.0 3.6 %all-to-all-start.1 = ((bf16[8,512,128]{2,1,0:T(8,128)(2,1)}), bf16[8,512,128]{2,1,0:T(8,128)(2,1)S(1)}, u32[]{:S(2)}, u32[]{:S(2)}) async-start(bf16[8,512,128]{2,1,0:T(8,128)(2,1)} %bitcast.21), calls=%async_computation.1 | async-start | bytes 2097152 | tf_op jit(solution)/shard_map/all_to_all | solution.py:220
  31.6 0.9 collective-permute-done.3
  32.5 0.6 collective-permute-start.4
  33.0 0.0 collective-permute-start
  33.1 5.8 %collective-permute-done.4 = bf16[2,4,2,64,128]{4,3,2,1,0:T(8,128)(2,1)S(1)} collective-permute-done((bf16[2,4,2,64,128]{4,3,2,1,0:T(8,128)(2,1)S(1)}, bf16[2,4,2,64,128]{4,3,2,1,0:T(8,128)(2,1)S(1)}, u32[]{:S(2)}, u32[]{:S(2)}) %collective-permute-start.4) | collective-permute-done | bytes 262176 | tf_op jit(solution)/shard_map/ppermute | solution.py:212
  38.9 2.2 %collective-permute-done.2.refs_6_ = bf16[4,4,2,64,128]{4,3,2,1,0:T(8,128)(2,1)S(1)} collective-permute-done((bf16[4,4,2,64,128]{4,3,2,1,0:T(8,128)(2,1)S(1)}, bf16[4,4,2,64,128]{4,3,2,1,0:T(8,128)(2,1)S(1)}, u32[]{:S(2)}, u32[]{:S(2)}) %collective-permute-start.2) | collective-permute-done | bytes 524320 | tf_op jit(solution)/shard_map/ppermute | solution.py:208
  41.0 0.1 collective-permute-done.1.refs_4_
  41.2 0.1 collective-permute-start.7
  41.3 0.5 collective-permute-start.5
  41.8 0.1 collective-permute-start.6
  41.9 0.1 stack.40.refs_0_
  41.9 0.0 collective-permute-done.refs_3_
  41.9 3.4 %all-to-all-done.1 = bf16[8,512,128]{2,1,0:T(8,128)(2,1)S(1)} async-done(((bf16[8,512,128]{2,1,0:T(8,128)(2,1)}), bf16[8,512,128]{2,1,0:T(8,128)(2,1)S(1)}, u32[]{:S(2)}, u32[]{:S(2)}) %all-to-all-start.1) | async-done | bytes 1048608 | tf_op jit(solution)/shard_map/all_to_all | solution.py:220
  45.4 0.0 collective-permute-done.7.refs_9_
  45.4 102.8 %shard_map.39 = bf16[8,64,1024]{2,1,0:T(8,128)(2,1)S(1)} custom-call(s32[10]{0:T(128)S(1)} %stack.40.refs_0_, bf16[4,1024,128]{2,1,0:T(8,128)(2,1)S(1)} %bitcast.20, bf16[4,4,2,64,128]{4,3,2,1,0:T(8,128)(2,1)S(1)} %bitcast.19, bf16[4,4,2,64,128]{4,3,2,1,0:T(8,128)(2,1)} %collective-permute-done.refs_3_, ...), custom_call_target="tpu_custom_call" | custom-call | flops 20000000000 | bytes 6291456 | tf_op jit(solution)/shard_map/pallas_call | solution.py:191
  148.2 16.0 %all_to_all.15 = bf16[8,64,1024]{2,1,0:T(8,128)(2,1)S(1)} all-to-all(bf16[8,64,1024]{2,1,0:T(8,128)(2,1)S(1)} %shard_map.39), channel_id=1, replica_groups={{0,24,32,56,64,88,96,120},{8,16,40,48,72,80,104,112},{1,25,33,57,65,89,..., dimensions={0} | all-to-all | bytes 2097152 | tf_op jit(solution)/shard_map/all_to_all | solution.py:220
  164.1 1.1 copy.5
  (5 shorter events, 0.1 us)
Async XLA Ops:
  2.0 19.6 %all-to-all-start = ((bf16[16,2,64,128]{3,2,1,0:T(8,128)(2,1)}), bf16[16,2,64,128]{3,2,1,0:T(8,128)(2,1)S(1)}, u32[]{:S(2)}, u32[]{:S(2)}) async-start(bf16[16,2,64,128]{3,2,1,0:T(8,128)(2,1)} %shard_map.38), calls=%async_computation | async-start | bytes 1048576 | tf_op jit(solution)/shard_map/all_to_all | solution.py:226
  21.6 10.8 %collective-permute-start.3 = (bf16[2,4,2,64,128]{4,3,2,1,0:T(8,128)(2,1)S(1)}, bf16[2,4,2,64,128]{4,3,2,1,0:T(8,128)(2,1)S(1)}, u32[]{:S(2)}, u32[]{:S(2)}) collective-permute-start(bf16[2,4,2,64,128]{4,3,2,1,0:T(8,128)(2,1)S(1)} %bitcast.23), channel_id=1, source_target_pairs={{4,0},{5,1},{6,2},{7,3},{0,4},{1,5},{2,6},{3,7},{12,8},{13,9},{14,... | collective-permute-start | bytes 786440 | tf_op jit(solution)/shard_map/ppermute | solution.py:208
  24.8 16.3 %collective-permute-start.2 = (bf16[4,4,2,64,128]{4,3,2,1,0:T(8,128)(2,1)S(1)}, bf16[4,4,2,64,128]{4,3,2,1,0:T(8,128)(2,1)S(1)}, u32[]{:S(2)}, u32[]{:S(2)}) collective-permute-start(bf16[4,4,2,64,128]{4,3,2,1,0:T(8,128)(2,1)S(1)} %bitcast.16), channel_id=1, source_target_pairs={{6,0},{7,1},{0,2},{1,3},{2,4},{3,5},{4,6},{5,7},{14,8},{15,9},{8,1... | collective-permute-start | bytes 1572872 | tf_op jit(solution)/shard_map/ppermute | solution.py:208
  25.3 15.8 %collective-permute-start.1 = (bf16[4,4,2,64,128]{4,3,2,1,0:T(8,128)(2,1)S(1)}, bf16[4,4,2,64,128]{4,3,2,1,0:T(8,128)(2,1)S(1)}, u32[]{:S(2)}, u32[]{:S(2)}) collective-permute-start(bf16[4,4,2,64,128]{4,3,2,1,0:T(8,128)(2,1)S(1)} %bitcast.17), channel_id=1, source_target_pairs={{2,0},{3,1},{4,2},{5,3},{6,4},{7,5},{0,6},{1,7},{10,8},{11,9},{12,... | collective-permute-start | bytes 1572872 | tf_op jit(solution)/shard_map/ppermute | solution.py:208
  28.0 17.4 %all-to-all-start.1 = ((bf16[8,512,128]{2,1,0:T(8,128)(2,1)}), bf16[8,512,128]{2,1,0:T(8,128)(2,1)S(1)}, u32[]{:S(2)}, u32[]{:S(2)}) async-start(bf16[8,512,128]{2,1,0:T(8,128)(2,1)} %bitcast.21), calls=%async_computation.1 | async-start | bytes 2097152 | tf_op jit(solution)/shard_map/all_to_all | solution.py:220
  32.5 6.4 %collective-permute-start.4 = (bf16[2,4,2,64,128]{4,3,2,1,0:T(8,128)(2,1)S(1)}, bf16[2,4,2,64,128]{4,3,2,1,0:T(8,128)(2,1)S(1)}, u32[]{:S(2)}, u32[]{:S(2)}) collective-permute-start(bf16[2,4,2,64,128]{4,3,2,1,0:T(8,128)(2,1)S(1)} %collective-permute-done.3), channel_id=1, source_target_pairs={{8,0},{0,8},{24,16},{16,24},{40,32},{32,40},{56,48},{48,56},{72,64... | collective-permute-start | bytes 786440 | tf_op jit(solution)/shard_map/ppermute | solution.py:212
  33.0 8.9 %collective-permute-start = (bf16[4,4,2,64,128]{4,3,2,1,0:T(8,128)(2,1)S(1)}, bf16[4,4,2,64,128]{4,3,2,1,0:T(8,128)(2,1)}, u32[]{:S(2)}, u32[]{:S(2)}) collective-permute-start(bf16[4,4,2,64,128]{4,3,2,1,0:T(8,128)(2,1)S(1)} %bitcast.18), channel_id=1, source_target_pairs={{1,0},{0,1},{3,2},{2,3},{5,4},{4,5},{7,6},{6,7},{9,8},{8,9},{11,10... | collective-permute-start | bytes 1572872 | tf_op jit(solution)/shard_map/ppermute | solution.py:216
  41.2 4.2 %collective-permute-start.7 = (bf16[4,4,2,64,128]{4,3,2,1,0:T(8,128)(2,1)S(1)}, bf16[4,4,2,64,128]{4,3,2,1,0:T(8,128)(2,1)}, u32[]{:S(2)}, u32[]{:S(2)}) collective-permute-start(bf16[4,4,2,64,128]{4,3,2,1,0:T(8,128)(2,1)S(1)} %constant_dynamic-update-slice_fusion.refs_8_), channel_id=1, source_target_pairs={{1,0},{0,1},{3,2},{2,3},{5,4},{4,5},{7,6},{6,7},{9,8},{8,9},{11,10... | collective-permute-start | bytes 1572872 | tf_op jit(solution)/shard_map/ppermute | solution.py:216
  41.3 4.1 %collective-permute-start.5 = (bf16[4,4,2,64,128]{4,3,2,1,0:T(8,128)(2,1)S(1)}, bf16[4,4,2,64,128]{4,3,2,1,0:T(8,128)(2,1)}, u32[]{:S(2)}, u32[]{:S(2)}) collective-permute-start(bf16[4,4,2,64,128]{4,3,2,1,0:T(8,128)(2,1)S(1)} %collective-permute-done.1.refs_4_), channel_id=1, source_target_pairs={{1,0},{0,1},{3,2},{2,3},{5,4},{4,5},{7,6},{6,7},{9,8},{8,9},{11,10... | collective-permute-start | bytes 1572872 | tf_op jit(solution)/shard_map/ppermute | solution.py:216
  41.8 3.6 %collective-permute-start.6 = (bf16[4,4,2,64,128]{4,3,2,1,0:T(8,128)(2,1)S(1)}, bf16[4,4,2,64,128]{4,3,2,1,0:T(8,128)(2,1)}, u32[]{:S(2)}, u32[]{:S(2)}) collective-permute-start(bf16[4,4,2,64,128]{4,3,2,1,0:T(8,128)(2,1)S(1)} %collective-permute-done.2.refs_6_), channel_id=1, source_target_pairs={{1,0},{0,1},{3,2},{2,3},{5,4},{4,5},{7,6},{6,7},{9,8},{8,9},{11,10... | collective-permute-start | bytes 1572872 | tf_op jit(solution)/shard_map/ppermute | solution.py:216

commit v6 on v4

--- a/solution.py
+++ b/solution.py
@@ -243,9 +243,11 @@
     inner = (z == 1) | (z == 2)
     half = around(jnp.where(inner, own[2:], own[:2]), 2)
     rest = across(half)
+    near = [around(own, step) for step in (1, 3)]
+    near[0], near[1], rest = lax.optimization_barrier((near[0], near[1], rest))
     far = jnp.concatenate([jnp.where(inner, rest, half), jnp.where(inner, half, rest)], axis=0)
     blocks, slots = [own, other], [xc, xc ^ 1]
-    for step, block in ((1, around(own, 1)), (3, around(own, 3)), (2, far)):
+    for step, block in ((1, near[0]), (3, near[1]), (2, far)):
         blocks += [block, swap(block)]
         slots += [(xc + 2 * step) % 8, (xc + 2 * step) % 8 ^ 1]
     where = jnp.stack([jnp.where(inner, 1, 0), xc] + slots).astype(jnp.int32)

time: 169 us -> 169 us (level)
  no operation moved by 1% of the time
where the time goes in v6:
time: 169 us; the launch traced here: 168 us
  Pallas kernels  107 us (63%)
  waiting for transfers between devices  23.7 us (14%)
  starting transfers between devices  19.4 us (11%)
  blocking collectives  16.1 us (10%)
  local copies, waits for them, and re-layouts  1.73 us (1%)
    pallas_call x1, Pallas kernels, attend(): pl.pallas_call(attend_kernel, out_shape=jax.ShapeDtypeStruct((8, TOK, GRO...  103 us
    all_to_all x1, blocking collectives, trade(): lax.all_to_all(array, 'yz', split_axis=0, concat_axis=0, tiled=True, axis...  16.1 us
    all_to_all x1, waiting for transfers between devices, on_device(): own = lax.all_to_all(kv, 'yz', split_axis=0, concat_axis=0, tiled=True)  9.09 us
    all_to_all x1, starting transfers between devices, on_device(): own = lax.all_to_all(kv, 'yz', split_axis=0, concat_axis=0, tiled=True)  8.13 us
    ppermute x3, starting transfers between devices, around(): lax.ppermute(array, 'xc', [((n + 2 * step) % 8, n) for n in range(8)])  6.34 us
    all_to_all x1, waiting for transfers between devices, trade(): lax.all_to_all(array, 'yz', split_axis=0, concat_axis=0, tiled=True, axis...  6.3 us
    ppermute x3, waiting for transfers between devices, around(): lax.ppermute(array, 'xc', [((n + 2 * step) % 8, n) for n in range(8)])  6.18 us
    all_to_all x1, starting transfers between devices, trade(): lax.all_to_all(array, 'yz', split_axis=0, concat_axis=0, tiled=True, axis...  3.56 us
  transfers between devices with their start and end apart: 10, of which 6 were waited for; matrix products, arithmetic and copies ran while one was open for 0% of the time, Pallas kernels for 1%

profile of v6, /device:TPU:0, one launch (start us, length us, event | category | flops | bytes accessed | tf_op | source)
XLA Modules:
  0.0 168.2 jit_solution(17972871385266019734)
XLA Ops:
  0.0 2.0 %shard_map.38 = bf16[16,2,64,128]{3,2,1,0:T(8,128)(2,1)} custom-call(bf16[64,1024]{1,0:T(8,128)(2,1)} %k_ref.1, bf16[64,1024]{1,0:T(8,128)(2,1)} %v_ref.1), custom_call_target="tpu_custom_call" | custom-call | tf_op jit(solution)/shard_map/pallas_call | solution.py:42
  2.0 8.1 %all-to-all-start = ((bf16[16,2,64,128]{3,2,1,0:T(8,128)(2,1)}), bf16[16,2,64,128]{3,2,1,0:T(8,128)(2,1)S(1)}, u32[]{:S(2)}, u32[]{:S(2)}) async-start(bf16[16,2,64,128]{3,2,1,0:T(8,128)(2,1)} %shard_map.38), calls=%async_computation | async-start | bytes 1048576 | tf_op jit(solution)/shard_map/all_to_all | solution.py:237
  10.2 2.4 %shard_map.37 = bf16[64,64,128]{2,1,0:T(8,128)(2,1)} custom-call(bf16[64,8192]{1,0:T(8,128)(2,1)} %q_ref.1), custom_call_target="tpu_custom_call" | custom-call | tf_op jit(solution)/shard_map/pallas_call | solution.py:55
  12.5 9.1 %all-to-all-done = bf16[16,2,64,128]{3,2,1,0:T(8,128)(2,1)S(1)} async-done(((bf16[16,2,64,128]{3,2,1,0:T(8,128)(2,1)}), bf16[16,2,64,128]{3,2,1,0:T(8,128)(2,1)S(1)}, u32[]{:S(2)}, u32[]{:S(2)}) %all-to-all-start) | async-done | bytes 524320 | tf_op jit(solution)/shard_map/all_to_all | solution.py:237
  21.7 3.1 %collective-permute-start.3 = (bf16[2,4,2,64,128]{4,3,2,1,0:T(8,128)(2,1)S(1)}, bf16[2,4,2,64,128]{4,3,2,1,0:T(8,128)(2,1)S(1)}, u32[]{:S(2)}, u32[]{:S(2)}) collective-permute-start(bf16[2,4,2,64,128]{4,3,2,1,0:T(8,128)(2,1)S(1)} %bitcast.26), channel_id=1, source_target_pairs={{4,0},{5,1},{6,2},{7,3},{0,4},{1,5},{2,6},{3,7},{12,8},{13,9},{14,... | collective-permute-start | bytes 786440 | tf_op jit(solution)/shard_map/ppermute | solution.py:219
  24.8 0.6 collective-permute-start.2
  25.4 2.6 %collective-permute-start.1 = (bf16[4,4,2,64,128]{4,3,2,1,0:T(8,128)(2,1)S(1)}, bf16[4,4,2,64,128]{4,3,2,1,0:T(8,128)(2,1)S(1)}, u32[]{:S(2)}, u32[]{:S(2)}) collective-permute-start(bf16[4,4,2,64,128]{4,3,2,1,0:T(8,128)(2,1)S(1)} %bitcast.19), channel_id=1, source_target_pairs={{2,0},{3,1},{4,2},{5,3},{6,4},{7,5},{0,6},{1,7},{10,8},{11,9},{12,... | collective-permute-start | bytes 1572872 | tf_op jit(solution)/shard_map/ppermute | solution.py:219
  28.0 0.6 slice_bitcast_fusion.token_ref
  28.6 3.9 %collective-permute-done.3 = bf16[2,4,2,64,128]{4,3,2,1,0:T(8,128)(2,1)S(1)} collective-permute-done((bf16[2,4,2,64,128]{4,3,2,1,0:T(8,128)(2,1)S(1)}, bf16[2,4,2,64,128]{4,3,2,1,0:T(8,128)(2,1)S(1)}, u32[]{:S(2)}, u32[]{:S(2)}) %collective-permute-start.3) | collective-permute-done | bytes 262176 | tf_op jit(solution)/shard_map/ppermute | solution.py:219
  32.5 0.6 collective-permute-start.4
  33.1 3.6 %all-to-all-start.1 = ((bf16[8,512,128]{2,1,0:T(8,128)(2,1)}), bf16[8,512,128]{2,1,0:T(8,128)(2,1)S(1)}, u32[]{:S(2)}, u32[]{:S(2)}) async-start(bf16[8,512,128]{2,1,0:T(8,128)(2,1)} %shard_map.39), calls=%async_computation.1 | async-start | bytes 2097152 | tf_op jit(solution)/shard_map/all_to_all | solution.py:231
  36.6 0.1 collective-permute-start
  36.7 2.1 %collective-permute-done.4 = bf16[2,4,2,64,128]{4,3,2,1,0:T(8,128)(2,1)S(1)} collective-permute-done((bf16[2,4,2,64,128]{4,3,2,1,0:T(8,128)(2,1)S(1)}, bf16[2,4,2,64,128]{4,3,2,1,0:T(8,128)(2,1)S(1)}, u32[]{:S(2)}, u32[]{:S(2)}) %collective-permute-start.4) | collective-permute-done | bytes 262176 | tf_op jit(solution)/shard_map/ppermute | solution.py:223
  38.9 2.2 %collective-permute-done.2.refs_6_ = bf16[4,4,2,64,128]{4,3,2,1,0:T(8,128)(2,1)S(1)} collective-permute-done((bf16[4,4,2,64,128]{4,3,2,1,0:T(8,128)(2,1)S(1)}, bf16[4,4,2,64,128]{4,3,2,1,0:T(8,128)(2,1)S(1)}, u32[]{:S(2)}, u32[]{:S(2)}) %collective-permute-start.2) | collective-permute-done | bytes 524320 | tf_op jit(solution)/shard_map/ppermute | solution.py:219
  41.1 0.1 collective-permute-done.1.refs_4_
  41.3 0.1 collective-permute-start.7
  41.3 0.5 collective-permute-start.5
  41.8 0.1 collective-permute-start.6
  41.9 0.1 stack.40.refs_0_
  42.0 0.0 collective-permute-done.refs_3_
  42.0 6.3 %all-to-all-done.1 = bf16[8,512,128]{2,1,0:T(8,128)(2,1)S(1)} async-done(((bf16[8,512,128]{2,1,0:T(8,128)(2,1)}), bf16[8,512,128]{2,1,0:T(8,128)(2,1)S(1)}, u32[]{:S(2)}, u32[]{:S(2)}) %all-to-all-start.1) | async-done | bytes 1048608 | tf_op jit(solution)/shard_map/all_to_all | solution.py:231
  48.3 102.7 %shard_map.40 = bf16[8,64,1024]{2,1,0:T(8,128)(2,1)S(1)} custom-call(s32[10]{0:T(128)S(1)} %stack.40.refs_0_, bf16[4,1024,128]{2,1,0:T(8,128)(2,1)S(1)} %bitcast.23, bf16[4,4,2,64,128]{4,3,2,1,0:T(8,128)(2,1)S(1)} %bitcast.22, bf16[4,4,2,64,128]{4,3,2,1,0:T(8,128)(2,1)} %collective-permute-done.refs_3_, ...), custom_call_target="tpu_custom_call" | custom-call | flops 20000000000 | bytes 6291456 | tf_op jit(solution)/shard_map/pallas_call | solution.py:202
  151.1 16.1 %all_to_all.15 = bf16[8,64,1024]{2,1,0:T(8,128)(2,1)S(1)} all-to-all(bf16[8,64,1024]{2,1,0:T(8,128)(2,1)S(1)} %shard_map.40), channel_id=1, replica_groups={{0,24,32,56,64,88,96,120},{8,16,40,48,72,80,104,112},{1,25,33,57,65,89,..., dimensions={0} | all-to-all | bytes 2097152 | tf_op jit(solution)/shard_map/all_to_all | solution.py:231
  167.1 1.1 copy.6
  (7 shorter events, 0.1 us)
Async XLA Ops:
  2.0 19.6 %all-to-all-start = ((bf16[16,2,64,128]{3,2,1,0:T(8,128)(2,1)}), bf16[16,2,64,128]{3,2,1,0:T(8,128)(2,1)S(1)}, u32[]{:S(2)}, u32[]{:S(2)}) async-start(bf16[16,2,64,128]{3,2,1,0:T(8,128)(2,1)} %shard_map.38), calls=%async_computation | async-start | bytes 1048576 | tf_op jit(solution)/shard_map/all_to_all | solution.py:237
  21.7 10.8 %collective-permute-start.3 = (bf16[2,4,2,64,128]{4,3,2,1,0:T(8,128)(2,1)S(1)}, bf16[2,4,2,64,128]{4,3,2,1,0:T(8,128)(2,1)S(1)}, u32[]{:S(2)}, u32[]{:S(2)}) collective-permute-start(bf16[2,4,2,64,128]{4,3,2,1,0:T(8,128)(2,1)S(1)} %bitcast.26), channel_id=1, source_target_pairs={{4,0},{5,1},{6,2},{7,3},{0,4},{1,5},{2,6},{3,7},{12,8},{13,9},{14,... | collective-permute-start | bytes 786440 | tf_op jit(solution)/shard_map/ppermute | solution.py:219
  24.8 16.3 %collective-permute-start.2 = (bf16[4,4,2,64,128]{4,3,2,1,0:T(8,128)(2,1)S(1)}, bf16[4,4,2,64,128]{4,3,2,1,0:T(8,128)(2,1)S(1)}, u32[]{:S(2)}, u32[]{:S(2)}) collective-permute-start(bf16[4,4,2,64,128]{4,3,2,1,0:T(8,128)(2,1)S(1)} %bitcast.18), channel_id=1, source_target_pairs={{6,0},{7,1},{0,2},{1,3},{2,4},{3,5},{4,6},{5,7},{14,8},{15,9},{8,1... | collective-permute-start | bytes 1572872 | tf_op jit(solution)/shard_map/ppermute | solution.py:219
  25.4 15.8 %collective-permute-start.1 = (bf16[4,4,2,64,128]{4,3,2,1,0:T(8,128)(2,1)S(1)}, bf16[4,4,2,64,128]{4,3,2,1,0:T(8,128)(2,1)S(1)}, u32[]{:S(2)}, u32[]{:S(2)}) collective-permute-start(bf16[4,4,2,64,128]{4,3,2,1,0:T(8,128)(2,1)S(1)} %bitcast.19), channel_id=1, source_target_pairs={{2,0},{3,1},{4,2},{5,3},{6,4},{7,5},{0,6},{1,7},{10,8},{11,9},{12,... | collective-permute-start | bytes 1572872 | tf_op jit(solution)/shard_map/ppermute | solution.py:219
  32.5 6.4 %collective-permute-start.4 = (bf16[2,4,2,64,128]{4,3,2,1,0:T(8,128)(2,1)S(1)}, bf16[2,4,2,64,128]{4,3,2,1,0:T(8,128)(2,1)S(1)}, u32[]{:S(2)}, u32[]{:S(2)}) collective-permute-start(bf16[2,4,2,64,128]{4,3,2,1,0:T(8,128)(2,1)S(1)} %collective-permute-done.3), channel_id=1, source_target_pairs={{8,0},{0,8},{24,16},{16,24},{40,32},{32,40},{56,48},{48,56},{72,64... | collective-permute-start | bytes 786440 | tf_op jit(solution)/shard_map/ppermute | solution.py:223
  33.1 15.3 %all-to-all-start.1 = ((bf16[8,512,128]{2,1,0:T(8,128)(2,1)}), bf16[8,512,128]{2,1,0:T(8,128)(2,1)S(1)}, u32[]{:S(2)}, u32[]{:S(2)}) async-start(bf16[8,512,128]{2,1,0:T(8,128)(2,1)} %shard_map.39), calls=%async_computation.1 | async-start | bytes 2097152 | tf_op jit(solution)/shard_map/all_to_all | solution.py:231
  36.6 5.4 %collective-permute-start = (bf16[4,4,2,64,128]{4,3,2,1,0:T(8,128)(2,1)S(1)}, bf16[4,4,2,64,128]{4,3,2,1,0:T(8,128)(2,1)}, u32[]{:S(2)}, u32[]{:S(2)}) collective-permute-start(bf16[4,4,2,64,128]{4,3,2,1,0:T(8,128)(2,1)S(1)} %bitcast.21), channel_id=1, source_target_pairs={{1,0},{0,1},{3,2},{2,3},{5,4},{4,5},{7,6},{6,7},{9,8},{8,9},{11,10... | collective-permute-start | bytes 1572872 | tf_op jit(solution)/shard_map/ppermute | solution.py:227
  41.3 7.1 %collective-permute-start.7 = (bf16[4,4,2,64,128]{4,3,2,1,0:T(8,128)(2,1)S(1)}, bf16[4,4,2,64,128]{4,3,2,1,0:T(8,128)(2,1)}, u32[]{:S(2)}, u32[]{:S(2)}) collective-permute-start(bf16[4,4,2,64,128]{4,3,2,1,0:T(8,128)(2,1)S(1)} %pad_maximum_fusion.refs_8_), channel_id=1, source_target_pairs={{1,0},{0,1},{3,2},{2,3},{5,4},{4,5},{7,6},{6,7},{9,8},{8,9},{11,10... | collective-permute-start | bytes 1572872 | tf_op jit(solution)/shard_map/ppermute | solution.py:227
  41.3 7.0 %collective-permute-start.5 = (bf16[4,4,2,64,128]{4,3,2,1,0:T(8,128)(2,1)S(1)}, bf16[4,4,2,64,128]{4,3,2,1,0:T(8,128)(2,1)}, u32[]{:S(2)}, u32[]{:S(2)}) collective-permute-start(bf16[4,4,2,64,128]{4,3,2,1,0:T(8,128)(2,1)S(1)} %collective-permute-done.1.refs_4_), channel_id=1, source_target_pairs={{1,0},{0,1},{3,2},{2,3},{5,4},{4,5},{7,6},{6,7},{9,8},{8,9},{11,10... | collective-permute-start | bytes 1572872 | tf_op jit(solution)/shard_map/ppermute | solution.py:227
  41.8 6.5 %collective-permute-start.6 = (bf16[4,4,2,64,128]{4,3,2,1,0:T(8,128)(2,1)S(1)}, bf16[4,4,2,64,128]{4,3,2,1,0:T(8,128)(2,1)}, u32[]{:S(2)}, u32[]{:S(2)}) collective-permute-start(bf16[4,4,2,64,128]{4,3,2,1,0:T(8,128)(2,1)S(1)} %collective-permute-done.2.refs_6_), channel_id=1, source_target_pairs={{1,0},{0,1},{3,2},{2,3},{5,4},{4,5},{7,6},{6,7},{9,8},{8,9},{11,10... | collective-permute-start | bytes 1572872 | tf_op jit(solution)/shard_map/ppermute | solution.py:227
